TPU v7x, 128 devices: a whole 4x4x4 slice. The times are simulated.
128 devices in a mesh: cuts: 8 (over x, core), intra: 16 (over z, y).
Axes of the slice: x: 4, y: 4, z: 4, core: 2. Of those that a mesh axis runs over, the one named last changes fastest.
Arguments:
- partials: float32 [8, 16, 2, 256, 8192], P('cuts', 'intra'), may hold values from -5 to 5
- errors: float32 [8, 2, 256, 8192], P('cuts', None, None, 'intra'), may hold values from -6 to 6
- start_seed: int32 [2, 8192, 32], P(None, 'intra'), may hold values from 0 to 65520
Outputs:
- gradient: bfloat16 [2, 256, 8192], replicated
- new_error: float32 [8, 2, 256, 8192], P('cuts', None, None, 'intra')
All inputs are finite; a program needn't handle non-finite values.
Results may differ from a plain program's by a relative error of at most 0.001.
Values may be sent and summed in bfloat16 or wider, within the bound.
A program may use at most 128 MiB of HBM per device.

v0:
```python
import jax
import jax.numpy as jnp
from jax import lax
from jax.sharding import PartitionSpec as P


def orthonormal(left_factor):
    finished = []
    for column in range(left_factor.shape[-1]):
        vector = left_factor[..., column]
        for earlier in finished:
            vector = vector - jnp.sum(earlier * vector, axis=-1, keepdims=True) * earlier
        length = jnp.sqrt(jnp.sum(vector * vector, axis=-1, keepdims=True) + 1e-06)
        finished.append(vector / length)
    return jnp.stack(finished, axis=-1)


def body(partials, errors, start_seed):
    local_part = partials.reshape(partials.shape[2:])
    summed = lax.psum_scatter(local_part, "intra", scatter_dimension=2, tiled=True)
    merged = summed + errors[0]
    start = (start_seed.astype(jnp.float32) - 32760.0) * (1.0 / 18918.0)
    left = jnp.einsum("lrd,ldk->lrk", merged, start, precision=lax.Precision.HIGHEST)
    left = lax.psum(left, "cuts")
    basis = orthonormal(left)
    right = jnp.einsum("lrd,lrk->ldk", merged, basis, precision=lax.Precision.HIGHEST)
    right = lax.psum(right, "cuts") / lax.axis_size("cuts")
    approx = jnp.einsum("lrk,ldk->lrd", basis, right, precision=lax.Precision.HIGHEST)
    new_error = (merged - approx)[None]
    gradient = lax.all_gather(approx.astype(jnp.bfloat16), "intra", axis=2, tiled=True)
    return (gradient, new_error)


def solution(mesh):
    in_specs = (
        P("cuts", "intra", None, None, None),
        P("cuts", None, None, "intra"),
        P(None, "intra", None),
    )
    out_specs = (P(), P("cuts", None, None, "intra"))
    return jax.shard_map(body, mesh=mesh, in_specs=in_specs, out_specs=out_specs, check_vma=False)
```

profile of v0, /device:TPU:1, one launch (start us, length us, event | category | flops | bytes accessed | tf_op | source)
XLA Modules:
  0.0 399.0 jit_solution(17329455913091187820)
XLA Ops:
  7.9 117.0 %reduce-scatter.2.cloned.1.call-done = f32[2,256,512]{2,1,0:T(8,128)} async-done(((f32[2,256,8192]{2,1,0:T(8,128)}), f32[2,256,512]{2,1,0:T(8,128)}) %reduce-scatter.2.cloned.1.call-update) | async-done | bytes 1048592 | tf_op jit(solution)/shard_map/reduce_scatter | solution.py:20
  124.9 2.4 fusion.2
  128.1 56.5 %all-reduce.3.cloned.1.call-done = f32[2,256,32]{1,0,2:T(2,128)} async-done(((f32[2,256,32]{1,0,2:T(2,128)}), f32[2,256,32]{1,0,2:T(2,128)}) %all-reduce.3.cloned.1.call-update) | async-done | bytes 65552 | tf_op jit(solution)/shard_map/psum | solution.py:24
  185.4 1.2 fusion.12
  186.6 1.1 fusion.30
  187.7 0.8 multiply_reduce_fusion.495
  188.6 1.3 multiply_reduce_fusion.30
  189.9 1.1 multiply_reduce_fusion.440
  191.2 1.0 multiply_reduce_fusion.29
  192.3 1.0 multiply_reduce_fusion.241
  193.3 1.1 multiply_reduce_fusion.389
  228.6 0.8 constant_dynamic-update-slice_fusion.16
  230.2 0.8 constant_dynamic-update-slice_fusion.14
  231.0 0.8 constant_dynamic-update-slice_fusion.13
  231.8 0.8 constant_dynamic-update-slice_fusion.12
  232.6 0.8 constant_dynamic-update-slice_fusion.11
  233.4 0.8 constant_dynamic-update-slice_fusion.10
  234.3 0.8 constant_dynamic-update-slice_fusion.9
  235.1 0.8 constant_dynamic-update-slice_fusion.8
  235.9 0.8 constant_dynamic-update-slice_fusion.7
  236.8 0.9 constant_dynamic-update-slice_fusion.6
  237.6 0.9 constant_dynamic-update-slice_fusion.5
  238.5 0.9 constant_dynamic-update-slice_fusion.4
  239.4 0.9 constant_dynamic-update-slice_fusion.3
  240.2 0.9 constant_dynamic-update-slice_fusion.2
  241.1 0.9 constant_dynamic-update-slice_fusion.1
  242.0 0.9 constant_dynamic-update-slice_fusion
  242.8 1.4 fusion.9
  244.3 58.3 %all-reduce.5.cloned.1.call-done = f32[2,512,32]{1,2,0:T(8,128)} async-done(((f32[2,512,32]{1,2,0:T(8,128)}), f32[2,512,32]{1,2,0:T(8,128)}) %all-reduce.5.cloned.1.call-update) | async-done | bytes 131088 | tf_op jit(solution)/shard_map/psum | solution.py:27
  302.6 3.1 subtract_bitcast_fusion
  305.7 79.0 %all-gather.2.cloned.1.call-done = bf16[2,256,8192]{2,1,0:T(8,128)(2,1)} async-done(((bf16[2,256,512]{2,1,0:T(8,128)(2,1)}), bf16[2,256,8192]{2,1,0:T(8,128)(2,1)}) %all-gather.2.cloned.1.call-update) | async-done | bytes 8388624 | tf_op jit(solution)/shard_map/all_gather | solution.py:30
  384.7 7.8 %copy.513 = bf16[2,256,8192]{2,1,0:T(8,128)(2,1)} copy(bf16[2,256,8192]{2,1,0:T(8,128)(2,1)} %all-gather.2.cloned.1.call-done) | data formatting | bytes 16777216
  (146 shorter events, 37.4 us)
Async XLA Ops:
  7.2 117.8 %reduce-scatter.2.cloned.1.call-start = ((), (), s32[]{:S(2)}) async-start(), calls=%async_computation.1 | async-start | bytes 17825792 | tf_op jit(solution)/shard_map/reduce_scatter | solution.py:20
  7.2 117.7 %copy-start = (f32[1,2,256,512]{3,2,1,0:T(8,128)S(1)}, f32[1,2,256,512]{3,2,1,0:T(8,128)}, u32[]{:S(2)}) copy-start(f32[1,2,256,512]{3,2,1,0:T(8,128)} %param.4) | copy-start | bytes 3145732
  7.2 117.7 %copy-start.2 = (s32[2,512,32]{1,2,0:T(8,128)S(1)}, s32[2,512,32]{1,2,0:T(8,128)}, u32[]{:S(2)}) copy-start(s32[2,512,32]{1,2,0:T(8,128)} %param.5) | copy-start | bytes 393220
  7.9 176.7 %all-reduce.3.cloned.1.call-start = ((), (), s32[]{:S(2)}) async-start(), calls=%async_computation.2 | async-start | bytes 131072 | tf_op jit(solution)/shard_map/psum | solution.py:24
  124.9 117.9 %copy-start.1 = (f32[2,256,512]{2,1,0:T(8,128)S(1)}, f32[2,256,512]{2,1,0:T(8,128)}, u32[]{:S(2)}) copy-start(f32[2,256,512]{2,1,0:T(8,128)} %reduce-scatter.2.cloned.1.call-done) | copy-start | bytes 3145732
  128.1 174.5 %all-reduce.5.cloned.1.call-start = ((), (), s32[]{:S(2)}) async-start(), calls=%async_computation.3 | async-start | bytes 262144 | tf_op jit(solution)/shard_map/psum | solution.py:27
  244.3 140.4 %all-gather.2.cloned.1.call-start = ((), (), s32[]{:S(2)}) async-start(), calls=%async_computation.4 | async-start | bytes 8912896 | tf_op jit(solution)/shard_map/all_gather | solution.py:30
Sparse Core Ops, SparseCore 0:
  11.4 113.4 reduce-scatter.1
  128.2 56.3 all-reduce.2
  244.4 58.1 all-reduce.4
  305.9 78.7 all-gather.1
where the time goes:
time: 400 us; the launch traced here: 399 us
  waiting for transfers between devices  311 us (78%)
  other arithmetic  58 us (14%)
  between operations  14 us (4%)
  local copies, waits for them, and re-layouts  8.47 us (2%)
  matrix products  6.95 us (2%)
    reduce_scatter x1, waiting for transfers between devices, body(): lax.psum_scatter(local_part, 'intra', scatter_dimension=2, tiled=True)  117 us
    all_gather x1, waiting for transfers between devices, body(): lax.all_gather(approx.astype(jnp.bfloat16), 'intra', axis=2, tiled=True)  79 us
    psum x1, waiting for transfers between devices, body(): right = lax.psum(right, 'cuts') / lax.axis_size('cuts')  58.3 us
    psum x1, waiting for transfers between devices, body(): left = lax.psum(left, 'cuts')  56.5 us
    unnamed x31, other arithmetic  24.8 us
    reduce_sum x59, other arithmetic, orthonormal(): jnp.sum(earlier * vector, axis=-1, keepdims=True) * earlier  24.7 us
  transfers between devices with their start and end apart: 4, of which 4 were waited for; matrix products, arithmetic and copies ran while one was open for 0% of the time, Pallas kernels for 0%

commit v1 on v0

v1 whole, which is shorter than its diff:
```python
import functools

import jax
import jax.numpy as jnp
from jax import lax
from jax.experimental import pallas as pl
from jax.experimental.pallas import tpu as pltpu
from jax.sharding import PartitionSpec as P

MESH = pl.DeviceIdType.MESH
HIGHEST = lax.Precision.HIGHEST
STEPS = 8
LIMIT = 32767.0


def quantize(values):
    top = jnp.abs(values)
    while top.ndim > 2:
        top = jnp.max(top, axis=0)
    top = jnp.maximum(jnp.max(top, axis=0, keepdims=True), 1e-30)
    coded = jnp.round(values * (LIMIT / top)).astype(jnp.int32).astype(jnp.int16)
    return coded, top * (1.0 / LIMIT)


def restore(coded, scale):
    return coded.astype(jnp.int32).astype(jnp.float32) * scale


def exchange(part, errors, start, merged, basis_q, basis_s, right_q, right_s,
             own, error_v, send1, recv1, send2, recv2, sscale, rscale,
             left, left_all, vectors, basis, right, right_all, reduced, right_full,
             load_sem, error_sem, ssem, rsem, cut_send, cut_recv, plane_send, plane_recv, local_sem):
    cut = lax.axis_index("cuts")
    member = lax.axis_index("intra")
    y, z = lax.rem(member, 4), lax.div(member, 4)

    def wrap(v):
        return lax.rem(v + 8, 4)

    ring = (
        {"plus": (cut, z * 4 + wrap(y + 1)), "minus": (cut, z * 4 + wrap(y - 1)), "pos": y},
        {"plus": (cut, wrap(z + 1) * 4 + y), "minus": (cut, wrap(z - 1) * 4 + y), "pos": z},
    )

    def cut_peer(o):
        return lax.rem(cut + o, 8)

    def plane_peer(o):
        return lax.rem(member + o, 16)

    def load(g, _):
        for l in range(2):
            pltpu.make_async_copy(
                part.at[l, :, pl.ds(pl.multiple_of(g * 128, 128), 128)],
                own.at[l, lax.div(g, 16), lax.rem(lax.div(g, 4), 4), lax.rem(g, 4)],
                load_sem.at[l]).start()
        return 0

    lax.fori_loop(0, 64, load, 0)
    error_copy = pltpu.make_async_copy(errors, error_v, error_sem)
    error_copy.start()

    barrier = pltpu.get_barrier_semaphore()
    for o in range(1, 8):
        pl.semaphore_signal(barrier, inc=1, device_id=(cut_peer(o), member), device_id_type=MESH)
    for o in range(1, 16):
        pl.semaphore_signal(barrier, inc=1, device_id=(cut, plane_peer(o)), device_id_type=MESH)
    pl.semaphore_wait(barrier, 22)
    error_copy.wait()

    sends = (send1, send2)
    recvs = (recv1, recv2)

    def copies(t, s, p, m):
        axis = ring[s if p == 0 else 1 - s]
        to = axis["plus"] if m in (0, 2, 4) else axis["minus"]
        data = pltpu.make_async_remote_copy(
            src_ref=sends[p].at[t, s, m], dst_ref=recvs[p].at[t, s, m],
            send_sem=ssem.at[t, s, p, m, 0], recv_sem=rsem.at[t, s, p, m, 0],
            device_id=to, device_id_type=MESH)
        scale = pltpu.make_async_remote_copy(
            src_ref=sscale.at[t, s, p, m], dst_ref=rscale.at[t, s, p, m],
            send_sem=ssem.at[t, s, p, m, 1], recv_sem=rsem.at[t, s, p, m, 1],
            device_id=to, device_id_type=MESH)
        return data, scale

    def rows_of(t, s, h):
        return pl.ds(pl.multiple_of(lax.rem(t, 4) * 64 + s * 32 + h * 16, 16), 16)

    def term(t, s, p, q, h):
        l, rows = lax.div(t, 4), rows_of(t, s, h)
        if p == 0:
            return own[l, :, q, :, rows, :] if s == 0 else own[l, q, :, :, rows, :]
        return own[l, q, y, :, rows, :] if s == 0 else own[l, z, q, :, rows, :]

    def send(t, s, p, m, values):
        coded, scale = quantize(values)
        sends[p][t, s, m] = coded
        sscale[t, s, p, m] = scale
        for copy in copies(t, s, p, m):
            copy.start()

    def receive(t, s, p, m):
        for copy in copies(t, s, p, m):
            copy.wait_recv()
        return restore(recvs[p][t, s, m], rscale[t, s, p, m])

    def first(t, s, p):
        pos = ring[s if p == 0 else 1 - s]["pos"]
        send(t, s, p, 0, term(t, s, p, wrap(pos + 2), 0))
        send(t, s, p, 1, term(t, s, p, wrap(pos + 2), 1))
        send(t, s, p, 2, term(t, s, p, wrap(pos + 1), 1))
        send(t, s, p, 3, term(t, s, p, wrap(pos - 1), 0))

    def second(t, s, p):
        pos = ring[s if p == 0 else 1 - s]["pos"]
        send(t, s, p, 4, term(t, s, p, wrap(pos + 1), 0) + receive(t, s, p, 0))
        send(t, s, p, 5, term(t, s, p, wrap(pos - 1), 1) + receive(t, s, p, 1))

    def total(t, s, p, h):
        pos = ring[s if p == 0 else 1 - s]["pos"]
        pair = (3, 4) if h == 0 else (2, 5)
        return term(t, s, p, pos, h) + receive(t, s, p, pair[0]) + receive(t, s, p, pair[1])

    def step(t, _):
        @pl.when(t < STEPS)
        def _():
            @pl.when(lax.rem(t, 4) == 0)
            def _():
                l = lax.div(t, 4)
                pltpu.make_async_copy(own.at[l], own.at[l], load_sem.at[l]).wait()

            for s in range(2):
                first(t, s, 0)

        @pl.when((t >= 1) & (t < STEPS + 1))
        def _():
            for s in range(2):
                second(t - 1, s, 0)

        @pl.when((t >= 2) & (t < STEPS + 2))
        def _():
            u = t - 2
            l = lax.div(u, 4)
            for s in range(2):
                for h in range(2):
                    summed = total(u, s, 0, h)
                    if s == 0:
                        own[l, :, y, :, rows_of(u, s, h), :] = summed
                    else:
                        own[l, z, :, :, rows_of(u, s, h), :] = summed
                first(u, s, 1)

        @pl.when((t >= 3) & (t < STEPS + 3))
        def _():
            for s in range(2):
                second(t - 3, s, 1)

        @pl.when(t >= 4)
        def _():
            u = t - 4
            l = lax.div(u, 4)
            for s in range(2):
                for h in range(2):
                    rows = rows_of(u, s, h)
                    summed = total(u, s, 1, h)
                    wide = jnp.concatenate([summed[i] for i in range(4)], axis=1)
                    merged[l, rows, :] = wide + error_v[l, rows, :]

        return 0

    lax.fori_loop(0, STEPS + 4, step, 0)

    def cut_copy(kind, o, src, dst):
        return pltpu.make_async_remote_copy(
            src_ref=src, dst_ref=dst, send_sem=cut_send.at[kind, o], recv_sem=cut_recv.at[kind, o],
            device_id=(cut_peer(o), member), device_id_type=MESH)

    for l in range(2):
        left[l] = lax.dot_general(start[l], merged[l], (((1,), (1,)), ((), ())),
                                  precision=HIGHEST, preferred_element_type=jnp.float32)
    lefts = [cut_copy(0, o, left, left_all.at[cut]) for o in range(1, 8)]
    for copy in lefts:
        copy.start()
    left_all[cut] = left[...]
    for copy in lefts:
        copy.wait()
    summed_left = left_all[0]
    for c in range(1, 8):
        summed_left = summed_left + left_all[c]
    vectors[...] = summed_left

    later = lax.broadcasted_iota(jnp.int32, (32, 1), 0)

    def column(k, _):
        for l in range(2):
            v = vectors[l, pl.ds(k, 1), :]
            block = vectors[l]
            size = jnp.sum(v * v, axis=1, keepdims=True) + 1e-6
            dots = jnp.sum(block * v, axis=1, keepdims=True)
            basis[l, pl.ds(k, 1), :] = v / jnp.sqrt(size)
            vectors[l] = block - jnp.where(later > k, dots / size, 0.0) * v
        return 0

    lax.fori_loop(0, 32, column, 0)

    core = lax.rem(cut, 2)

    def plane_copies(o, which):
        there = (cut, plane_peer(o))
        return (
            [pltpu.make_async_remote_copy(
                src_ref=ref.at[core, member], dst_ref=ref.at[core, member],
                send_sem=plane_send.at[n, o], recv_sem=plane_recv.at[n, o],
                device_id=there, device_id_type=MESH)
             for n, ref in enumerate((basis_q, basis_s, right_q, right_s)) if n in which])

    coded, scale = quantize(basis[core])
    basis_q[core, member] = coded
    basis_s[core, member] = scale
    for o in range(1, 16):
        for copy in plane_copies(o, (0, 1)):
            copy.start()

    for l in range(2):
        wide = jnp.dot(basis[l], merged[l], precision=HIGHEST, preferred_element_type=jnp.float32)
        for i in range(4):
            right[l * 4 + i] = wide[:, i * 128:(i + 1) * 128]
    rights = [cut_copy(1, o, right.at[cut_peer(o)], right_all.at[cut]) for o in range(1, 8)]
    for copy in rights:
        copy.start()
    right_all[cut] = right[cut]
    for copy in rights:
        copy.wait()
    summed_right = right_all[0]
    for c in range(1, 8):
        summed_right = summed_right + right_all[c]
    reduced[...] = summed_right * 0.125
    gathers = [cut_copy(2, o, reduced, right_full.at[cut]) for o in range(1, 8)]
    for copy in gathers:
        copy.start()
    right_full[cut] = reduced[...]
    for copy in gathers:
        copy.wait()

    coded, scale = quantize(jnp.concatenate([right_full[core * 4 + i] for i in range(4)], axis=1))
    right_q[core, member] = coded
    right_s[core, member] = scale
    for o in range(1, 16):
        for copy in plane_copies(o, (2, 3)):
            copy.start()
    for o in range(1, 16):
        for copy in plane_copies(o, (0, 1, 2, 3)):
            copy.wait()

    sibling = (cut + 1 - 2 * core, member)
    swaps = [pltpu.make_async_remote_copy(
        src_ref=ref.at[core], dst_ref=ref.at[core], send_sem=local_sem.at[0, n], recv_sem=local_sem.at[1, n],
        device_id=sibling, device_id_type=MESH) for n, ref in enumerate((basis_q, basis_s, right_q, right_s))]
    for copy in swaps:
        copy.start()
    for copy in swaps:
        copy.wait()

    def drained(t, _):
        for s in range(2):
            for p in range(2):
                for m in range(6):
                    for copy in copies(t, s, p, m):
                        copy.wait_send()
        return 0

    lax.fori_loop(0, STEPS, drained, 0)


def decompress(member_ref, basis_q, basis_s, right_q, right_s, merged, gradient, new_error):
    j = pl.program_id(0)
    for l in range(2):
        b = restore(basis_q[l, 0], basis_s[l, 0])
        r = restore(right_q[l, 0], right_s[l, 0])
        b_high, r_high = b.astype(jnp.bfloat16), r.astype(jnp.bfloat16)
        b_low = (b - b_high.astype(jnp.float32)).astype(jnp.bfloat16)
        r_low = (r - r_high.astype(jnp.float32)).astype(jnp.bfloat16)
        approx = lax.dot_general(
            jnp.concatenate([b_high, b_high, b_low], axis=0),
            jnp.concatenate([r_high, r_low, r_high], axis=0),
            (((0,), (0,)), ((), ())), preferred_element_type=jnp.float32)
        gradient[l] = approx.astype(jnp.bfloat16)

        @pl.when(j == member_ref[0])
        def _():
            new_error[l] = merged[l] - approx


def body(partials, errors, start_seed):
    f32, i16 = jnp.float32, jnp.int16
    start = jnp.swapaxes((start_seed.astype(f32) - 32760.0) * (1.0 / 18918.0), 1, 2)
    vmem = pl.BlockSpec(memory_space=pltpu.VMEM)
    hbm = pl.BlockSpec(memory_space=pl.ANY)
    dma = pltpu.SemaphoreType.DMA
    merged, basis_q, basis_s, right_q, right_s = pl.pallas_call(
        exchange,
        out_shape=(
            jax.ShapeDtypeStruct((2, 256, 512), f32),
            jax.ShapeDtypeStruct((2, 16, 32, 256), i16),
            jax.ShapeDtypeStruct((2, 16, 1, 256), f32),
            jax.ShapeDtypeStruct((2, 16, 32, 512), i16),
            jax.ShapeDtypeStruct((2, 16, 1, 512), f32),
        ),
        in_specs=[hbm, hbm, vmem],
        out_specs=(vmem,) * 5,
        scratch_shapes=[
            pltpu.VMEM((2, 4, 4, 4, 256, 128), f32),
            pltpu.VMEM((2, 256, 512), f32),
            pltpu.VMEM((STEPS, 2, 6, 4, 4, 16, 128), i16),
            pltpu.VMEM((STEPS, 2, 6, 4, 4, 16, 128), i16),
            pltpu.VMEM((STEPS, 2, 6, 4, 16, 128), i16),
            pltpu.VMEM((STEPS, 2, 6, 4, 16, 128), i16),
            pltpu.VMEM((STEPS, 2, 2, 6, 1, 128), f32),
            pltpu.VMEM((STEPS, 2, 2, 6, 1, 128), f32),
            pltpu.VMEM((2, 32, 256), f32),
            pltpu.VMEM((8, 2, 32, 256), f32),
            pltpu.VMEM((2, 32, 256), f32),
            pltpu.VMEM((2, 32, 256), f32),
            pltpu.VMEM((8, 32, 128), f32),
            pltpu.VMEM((8, 32, 128), f32),
            pltpu.VMEM((32, 128), f32),
            pltpu.VMEM((8, 32, 128), f32),
            dma((2,)),
            dma,
            dma((STEPS, 2, 2, 6, 2)),
            dma((STEPS, 2, 2, 6, 2)),
            dma((3, 8)),
            dma((3, 8)),
            dma((4, 16)),
            dma((4, 16)),
            dma((2, 4)),
        ],
        compiler_params=pltpu.CompilerParams(
            collective_id=0, has_side_effects=True, vmem_limit_bytes=56 * 1024 * 1024),
        name="exchange",
    )(partials.reshape(2, 256, 8192), errors.reshape(2, 256, 512), start)

    member = lax.axis_index("intra").astype(jnp.int32).reshape(1)
    gradient, new_error = pl.pallas_call(
        decompress,
        grid=(16,),
        out_shape=(
            jax.ShapeDtypeStruct((2, 256, 8192), jnp.bfloat16),
            jax.ShapeDtypeStruct((2, 256, 512), f32),
        ),
        in_specs=[
            pl.BlockSpec(memory_space=pltpu.SMEM),
            pl.BlockSpec((2, 1, 32, 256), lambda j: (0, j, 0, 0)),
            pl.BlockSpec((2, 1, 1, 256), lambda j: (0, j, 0, 0)),
            pl.BlockSpec((2, 1, 32, 512), lambda j: (0, j, 0, 0)),
            pl.BlockSpec((2, 1, 1, 512), lambda j: (0, j, 0, 0)),
            pl.BlockSpec((2, 256, 512), lambda j: (0, 0, 0)),
        ],
        out_specs=(
            pl.BlockSpec((2, 256, 512), lambda j: (0, 0, j)),
            pl.BlockSpec((2, 256, 512), lambda j: (0, 0, 0)),
        ),
        compiler_params=pltpu.CompilerParams(vmem_limit_bytes=32 * 1024 * 1024),
        name="decompress",
    )(member, basis_q, basis_s, right_q, right_s, merged)
    return gradient, new_error[None]


def solution(mesh):
    in_specs = (
        P("cuts", "intra", None, None, None),
        P("cuts", None, None, "intra"),
        P(None, "intra", None),
    )
    out_specs = (P(), P("cuts", None, None, "intra"))
    return jax.shard_map(body, mesh=mesh, in_specs=in_specs, out_specs=out_specs, check_vma=False)
```

time: 400 us -> 126 us (0.32)
  waiting for transfers between devices: 311 us -> 0 us
  Pallas kernels: 0 us -> 119 us
  other arithmetic: 58 us -> 1.58 us
  between operations: 14 us -> 0.65 us
  matrix products: 6.95 us -> 0 us
    pallas_call x0 -> x2, Pallas kernels: none -> 119 us  [the longest x1 107 us: body(): pl.pallas_call(exchange, out_shape=(jax.ShapeDtypeStruct((2, 256, 512), f...]
    reduce_scatter x1 -> x0, waiting for transfers between devices: 117 us -> none  [body(): lax.psum_scatter(local_part, 'intra', scatter_dimension=2, tiled=True)]
    psum x2 -> x0, waiting for transfers between devices: 115 us -> none  [the longest x1 58.3 us: body(): right = lax.psum(right, 'cuts') / lax.axis_size('cuts')]
    all_gather x1 -> x0, waiting for transfers between devices: 79 us -> none  [body(): lax.all_gather(approx.astype(jnp.bfloat16), 'intra', axis=2, tiled=True)]
    reduce_sum x91 -> x0, other arithmetic: 32 us -> none  [the longest x59 24.7 us: orthonormal(): jnp.sum(earlier * vector, axis=-1, keepdims=True) * earlier]
    unnamed x31 -> x0, other arithmetic: 24.8 us -> none
    dot_general x3 -> x0, matrix products: 6.95 us -> none  [the longest x1 3.12 us: body(): jnp.einsum('lrk,ldk->lrd', basis, right, precision=lax.Precision.HIGHEST)]
  transfers between devices with their start and end apart: 4 -> 0, of which waited for: 4 -> 0; matrix products, arithmetic and copies ran while one was open for 0% -> 0% of each run, Pallas kernels for 0% -> 0%
where the time goes in v1:
time: 126 us
  Pallas kernels  119 us (94%)
  local copies, waits for them, and re-layouts  5.08 us (4%)
  other arithmetic  1.58 us (1%)
    pallas_call x1, Pallas kernels, body(): pl.pallas_call(exchange, out_shape=(jax.ShapeDtypeStruct((2, 256, 512), f...  107 us
    pallas_call x1, Pallas kernels, body(): pl.pallas_call(decompress, grid=(16,), out_shape=(jax.ShapeDtypeStruct((2...  11.5 us
    unnamed x10, local copies, waits for them, and re-layouts  5.08 us

profile of v1, /device:TPU:1, one launch (start us, length us, event | category | flops | bytes accessed | tf_op | source)
XLA Modules:
  0.0 126.0 jit_solution(10129363804315105785)
XLA Ops:
  0.6 1.6 %multiply_bitcast_fusion.start = f32[2,32,512]{2,1,0:T(8,128)} fusion(s32[2,512,32]{1,2,0:T(8,128)} %param.5), kind=kLoop, calls=%fused_computation | loop fusion | flops 98304 | bytes 262144 | tf_op jit(solution)/shard_map/transpose | solution.py:297
  2.2 107.2 %exchange.1 = (f32[2,256,512]{2,1,0:T(8,128)}, s16[2,16,32,256]{3,2,1,0:T(8,128)(2,1)}, f32[2,16,1,256]{3,2,1,0:T(1,128)}, s16[2,16,32,512]{3,2,1,0:T(8,128)(2,1)}, f32[2,16,1,512]{3,2,1,0:T(1,128)}) custom-call(f32[2,256,8192]{2,1,0:T(8,128)} %bitcast.6, f32[2,256,512]{2,1,0:T(8,128)} %bitcast.7, f32[2,32,512]{2,1,0:T(8,128)} %multiply_bitcast_fusion.start), custom_call_target="tpu_custom_call" | custom-call | tf_op jit(solution)/shard_map/exchange/pallas_call | solution.py:301
  109.4 0.0 copy-start
  109.5 1.2 copy-done
  110.7 0.0 copy-start.1
  110.7 1.2 copy-done.1
  111.9 0.0 copy-start.2
  111.9 1.0 copy-done.2
  112.9 0.0 copy-start.3
  112.9 0.8 copy-done.3
  113.8 0.0 copy-start.4
  113.8 0.8 copy-done.4
  114.5 11.5 %decompress.1 = (bf16[2,256,8192]{2,1,0:T(8,128)(2,1)}, f32[2,256,512]{2,1,0:T(8,128)}) custom-call(s32[1]{0:T(128)} %bitcast.member_ref, s16[2,16,32,256]{3,2,1,0:T(8,128)(2,1)S(1)} %copy-done.2, f32[2,16,1,256]{3,2,1,0:T(1,128)S(1)} %copy-done.4, s16[2,16,32,512]{3,2,1,0:T(8,128)(2,1)S(1)} %copy-done.1, f32[2,16,1,512]{3,2,1,0:T(1,128)S(1)} %copy-done.3, ...), custom_call_target="tpu_custom_call" | custom-call | tf_op jit(solution)/shard_map/decompress/pallas_call | solution.py:345
Async XLA Ops:
  109.4 1.2 copy-start
  110.7 1.2 copy-start.1
  111.9 1.0 copy-start.2
  112.9 0.8 copy-start.3
  113.8 0.8 copy-start.4

commit v2 on v0

v2 whole, which is shorter than its diff:
```python
import functools

import jax
import jax.numpy as jnp
from jax import lax
from jax.experimental import pallas as pl
from jax.experimental.pallas import tpu as pltpu
from jax.sharding import PartitionSpec as P

MESH = pl.DeviceIdType.MESH
HIGHEST = lax.Precision.HIGHEST
STEPS = 8
LIMIT = 32767.0


def quantize(values):
    top = jnp.abs(values)
    while top.ndim > 2:
        top = jnp.max(top, axis=0)
    top = jnp.maximum(jnp.max(top, axis=0, keepdims=True), 1e-30)
    coded = jnp.round(values * (LIMIT / top)).astype(jnp.int32).astype(jnp.int16)
    return coded, top * (1.0 / LIMIT)


def restore(coded, scale):
    return coded.astype(jnp.int32).astype(jnp.float32) * scale


def exchange(part, errors, seed, merged_out, basis_q, basis_s, right_q, right_s,
             own, error_v, merged, start,
             sa1, sb1, sa2, sb2, ra1, rb1, ra2, rb2, ssa, ssb, rsa, rsb,
             left, left_all, basis, right, right_all, right_full,
             basis_send, right_send, scale_send,
             load_sem, error_sem, out_sem, send_sem, recv_sem, cut_send, cut_recv,
             plane_send, plane_recv, swap_sem):
    cut = lax.axis_index("cuts")
    member = lax.axis_index("intra")
    y, z = lax.rem(member, 4), lax.div(member, 4)
    core = lax.rem(cut, 2)

    def wrap(v):
        return lax.rem(v + 8, 4)

    ring = (
        {"plus": (cut, z * 4 + wrap(y + 1)), "minus": (cut, z * 4 + wrap(y - 1)), "pos": y},
        {"plus": (cut, wrap(z + 1) * 4 + y), "minus": (cut, wrap(z - 1) * 4 + y), "pos": z},
    )

    def cut_peer(o):
        return lax.rem(cut + o, 8)

    def plane_peer(o):
        return lax.rem(member + o, 16)

    def load(l, first, count, sem):
        rows = pl.ds(first, count)

        def group(g, _):
            pltpu.make_async_copy(
                part.at[l, rows, pl.ds(pl.multiple_of(g * 128, 128), 128)],
                own.at[l, lax.div(g, 16), lax.rem(lax.div(g, 4), 4), lax.rem(g, 4), rows],
                load_sem.at[sem]).start()
            return 0

        lax.fori_loop(0, 64, group, 0)

    def loaded(l, first, count, sem):
        there = own.at[l, :, :, :, pl.ds(first, count)]
        pltpu.make_async_copy(there, there, load_sem.at[sem]).wait()

    load(0, 0, 64, 0)

    barrier = pltpu.get_barrier_semaphore()
    for o in range(1, 8):
        pl.semaphore_signal(barrier, inc=1, device_id=(cut_peer(o), member), device_id_type=MESH)
    for o in range(1, 16):
        pl.semaphore_signal(barrier, inc=1, device_id=(cut, plane_peer(o)), device_id_type=MESH)

    load(0, 64, 192, 1)
    error_copy = pltpu.make_async_copy(errors, error_v, error_sem)
    error_copy.start()
    load(1, 0, 256, 2)

    for l in range(2):
        start[l] = (seed[l].astype(jnp.float32) - 32760.0) * (1.0 / 18918.0)

    data_send, data_recv = ((sa1, sb1), (sa2, sb2)), ((ra1, rb1), (ra2, rb2))
    scale_slot = ((0, 0), (0, 2), (0, 1), (0, 3), (1, 0), (1, 1))

    def data_copy(t, s, p, m):
        axis = ring[s if p == 0 else 1 - s]
        g, n = (0, m) if m < 2 else (1, m - 2)
        return pltpu.make_async_remote_copy(
            src_ref=data_send[p][g].at[t, s, n], dst_ref=data_recv[p][g].at[t, s, n],
            send_sem=send_sem.at[p, g], recv_sem=recv_sem.at[t, p, g, 0],
            device_id=axis["plus"] if m % 2 == 0 else axis["minus"], device_id_type=MESH)

    def scale_copy(t, s, p, g, side):
        axis = ring[s if p == 0 else 1 - s]
        rows = pl.ds(side * 2, 2) if g == 0 else pl.ds(side, 1)
        there, here = (rsa, ssa) if g == 0 else (rsb, ssb)
        return pltpu.make_async_remote_copy(
            src_ref=here.at[t, p, s, rows], dst_ref=there.at[t, p, s, rows],
            send_sem=send_sem.at[2, g], recv_sem=recv_sem.at[t, p, g, 1],
            device_id=axis["plus"] if side == 0 else axis["minus"], device_id_type=MESH)

    def arrived(t, p, g):
        there = data_recv[p][g].at[t]
        pltpu.make_async_copy(there, there, recv_sem.at[t, p, g, 0]).wait()
        there = (rsa, rsb)[g].at[t, p]
        pltpu.make_async_copy(there, there, recv_sem.at[t, p, g, 1]).wait()

    def rows_of(t, s, h):
        return pl.ds(pl.multiple_of(lax.rem(t, 4) * 64 + s * 32 + h * 16, 16), 16)

    def term(t, s, p, q, h):
        l, rows = lax.div(t, 4), rows_of(t, s, h)
        if p == 0:
            return own[l, :, q, :, rows, :] if s == 0 else own[l, q, :, :, rows, :]
        return own[l, q, y, :, rows, :] if s == 0 else own[l, z, q, :, rows, :]

    def code(t, s, p, m, values):
        coded, scale = quantize(values)
        g, n = (0, m) if m < 2 else (1, m - 2)
        data_send[p][g][t, s, n] = coded
        group, row = scale_slot[m]
        (ssa, ssb)[group][t, p, s, row] = scale

    def got(t, s, p, m):
        g, n = (0, m) if m < 2 else (1, m - 2)
        group, row = scale_slot[m]
        return restore(data_recv[p][g][t, s, n], (rsa, rsb)[group][t, p, s, row])

    def first_code(t, s, p):
        pos = ring[s if p == 0 else 1 - s]["pos"]
        code(t, s, p, 0, term(t, s, p, wrap(pos + 2), 0))
        code(t, s, p, 1, term(t, s, p, wrap(pos + 2), 1))
        code(t, s, p, 2, term(t, s, p, wrap(pos + 1), 1))
        code(t, s, p, 3, term(t, s, p, wrap(pos - 1), 0))

    def first_send(t, s, p):
        for side in range(2):
            scale_copy(t, s, p, 0, side).start()
        for m in range(4):
            data_copy(t, s, p, m).start()

    def second(t, s, p):
        pos = ring[s if p == 0 else 1 - s]["pos"]
        code(t, s, p, 4, term(t, s, p, wrap(pos + 1), 0) + got(t, s, p, 0))
        code(t, s, p, 5, term(t, s, p, wrap(pos - 1), 1) + got(t, s, p, 1))
        for side in range(2):
            scale_copy(t, s, p, 1, side).start()
            data_copy(t, s, p, 4 + side).start()

    def total(t, s, p, h):
        pos = ring[s if p == 0 else 1 - s]["pos"]
        pair = (3, 4) if h == 0 else (2, 5)
        return term(t, s, p, pos, h) + got(t, s, p, pair[0]) + got(t, s, p, pair[1])

    def left_copy(l, half, o):
        return pltpu.make_async_remote_copy(
            src_ref=left.at[l, half], dst_ref=left_all.at[l, half, o],
            send_sem=cut_send.at[0], recv_sem=cut_recv.at[l, half],
            device_id=(cut_peer(o), member), device_id_type=MESH)

    loaded(0, 0, 64, 0)
    for s in range(2):
        first_code(0, s, 0)
    pl.semaphore_wait(barrier, 22)

    def step(t, _):
        @pl.when(t < STEPS)
        def _():
            for s in range(2):
                first_send(t, s, 0)

        @pl.when((t >= 1) & (t < STEPS + 1))
        def _():
            arrived(t - 1, 0, 0)
            for s in range(2):
                second(t - 1, s, 0)

        @pl.when((t >= 2) & (t < STEPS + 2))
        def _():
            u = t - 2
            l = lax.div(u, 4)
            arrived(u, 0, 1)
            for s in range(2):
                for h in range(2):
                    summed = total(u, s, 0, h)
                    if s == 0:
                        own[l, :, y, :, rows_of(u, s, h), :] = summed
                    else:
                        own[l, z, :, :, rows_of(u, s, h), :] = summed
                first_code(u, s, 1)
                first_send(u, s, 1)

        @pl.when((t >= 3) & (t < STEPS + 3))
        def _():
            arrived(t - 3, 1, 0)
            for s in range(2):
                second(t - 3, s, 1)

        @pl.when(t >= 4)
        def _():
            u = t - 4
            l = lax.div(u, 4)
            arrived(u, 1, 1)

            @pl.when(u == 0)
            def _():
                error_copy.wait()

            for s in range(2):
                for h in range(2):
                    rows = rows_of(u, s, h)
                    summed = total(u, s, 1, h)
                    wide = jnp.concatenate([summed[i] for i in range(4)], axis=1)
                    merged[l, rows, :] = wide + error_v[l, rows, :]

            @pl.when(lax.rem(u, 2) == 1)
            def _():
                half = lax.div(lax.rem(u, 4), 2)
                rows = pl.ds(pl.multiple_of(half * 128, 128), 128)
                left[l, half] = lax.dot_general(
                    start[l], merged[l, rows, :], (((1,), (1,)), ((), ())),
                    precision=HIGHEST, preferred_element_type=jnp.float32)
                for o in range(1, 8):
                    left_copy(l, half, o).start()
                left_all[l, half, 0] = left[l, half]

        @pl.when(t + 1 < STEPS)
        def _():
            @pl.when(t + 1 == 1)
            def _():
                loaded(0, 64, 192, 1)

            @pl.when(t + 1 == 4)
            def _():
                loaded(1, 0, 256, 2)

            for s in range(2):
                first_code(t + 1, s, 0)

        return 0

    lax.fori_loop(0, STEPS + 4, step, 0)

    merged_copy = pltpu.make_async_copy(merged, merged_out, out_sem.at[0])
    merged_copy.start()

    def slot(c):
        return lax.rem(cut - c + 8, 8)

    vectors = []
    for l in range(2):
        halves = []
        for half in range(2):
            there = left_all.at[l, half, pl.ds(1, 7)]
            pltpu.make_async_copy(there, there, cut_recv.at[l, half]).wait()
            summed = left_all[l, half, slot(0)]
            for c in range(1, 8):
                summed = summed + left_all[l, half, slot(c)]
            halves.append(summed)
        vectors.append(jnp.concatenate(halves, axis=1))

    later = lax.broadcasted_iota(jnp.int32, (32, 1), 0)
    for k in range(32):
        for l in range(2):
            v = vectors[l][k:k + 1, :]
            size = jnp.sum(v * v, axis=1, keepdims=True) + 1e-6
            dots = jnp.sum(vectors[l] * v, axis=1, keepdims=True)
            basis[l, k:k + 1, :] = v / jnp.sqrt(size)
            vectors[l] = vectors[l] - jnp.where(later > k, dots / size, 0.0) * v

    for l in range(2):
        wide = jnp.dot(basis[l], merged[l], precision=HIGHEST, preferred_element_type=jnp.float32)
        for i in range(4):
            right[l * 4 + i] = wide[:, i * 128:(i + 1) * 128]
    rights = [pltpu.make_async_remote_copy(
        src_ref=right.at[cut_peer(o)], dst_ref=right_all.at[o],
        send_sem=cut_send.at[1], recv_sem=cut_recv.at[2, 0],
        device_id=(cut_peer(o), member), device_id_type=MESH) for o in range(1, 8)]
    for copy in rights:
        copy.start()
    right_all[0] = right[cut]

    def plane_copy(n, o, src, dst):
        return pltpu.make_async_remote_copy(
            src_ref=src, dst_ref=dst, send_sem=plane_send.at[n], recv_sem=plane_recv.at[n],
            device_id=(cut, plane_peer(o)), device_id_type=MESH)

    both = jnp.concatenate([basis[0], basis[1]] * 2, axis=0).T
    coded, scale = quantize(both)
    basis_send[0] = coded[:128]
    basis_send[1] = coded[128:]
    scale_send[0] = scale
    for o in range(1, 16):
        plane_copy(0, o, basis_send.at[core], basis_q.at[core, o]).start()
        plane_copy(1, o, scale_send.at[0], basis_s.at[o]).start()
    mine = [pltpu.make_async_copy(basis_send, basis_q.at[:, 0], out_sem.at[1]),
            pltpu.make_async_copy(scale_send.at[0], basis_s.at[0], out_sem.at[2])]
    for copy in mine:
        copy.start()

    def landed(there, sem):
        pltpu.make_async_copy(there, there, sem).wait()

    landed(right_all.at[pl.ds(1, 7)], cut_recv.at[2, 0])
    summed = right_all[slot(0)]
    for c in range(1, 8):
        summed = summed + right_all[slot(c)]
    right_full[0] = summed * 0.125
    for o in range(1, 8):
        pltpu.make_async_remote_copy(
            src_ref=right_full.at[0], dst_ref=right_full.at[o],
            send_sem=cut_send.at[2], recv_sem=cut_recv.at[2, 1],
            device_id=(cut_peer(o), member), device_id_type=MESH).start()
    landed(right_full.at[pl.ds(1, 7)], cut_recv.at[2, 1])

    for l in range(2):
        coded, scale = quantize(jnp.stack([right_full[slot(l * 4 + i)] for i in range(4)]))
        right_send[l] = coded
        scale_send[1 + l] = scale
    for o in range(1, 16):
        plane_copy(2, o, right_send.at[core], right_q.at[core, o]).start()
        plane_copy(3, o, scale_send.at[pl.ds(1, 2)], right_s.at[o]).start()
    more = [pltpu.make_async_copy(right_send, right_q.at[:, 0], out_sem.at[3]),
            pltpu.make_async_copy(scale_send.at[pl.ds(1, 2)], right_s.at[0], out_sem.at[4])]
    for copy in more:
        copy.start()

    def swap(n, ref):
        there = ref.at[core, pl.ds(1, 15)]
        return pltpu.make_async_remote_copy(
            src_ref=there, dst_ref=there, send_sem=swap_sem.at[0, n], recv_sem=swap_sem.at[1, n],
            device_id=(cut + 1 - 2 * core, member), device_id_type=MESH)

    landed(basis_q.at[core, pl.ds(1, 15)], plane_recv.at[0])
    swap(0, basis_q).start()
    landed(basis_s.at[pl.ds(1, 15)], plane_recv.at[1])
    landed(right_s.at[pl.ds(1, 15)], plane_recv.at[3])
    landed(right_q.at[core, pl.ds(1, 15)], plane_recv.at[2])
    swap(1, right_q).start()

    for p in range(2):
        for g in range(2):
            landed(data_send[p][g], send_sem.at[p, g])
    landed(ssa, send_sem.at[2, 0])
    landed(ssb, send_sem.at[2, 1])
    landed(left_all.at[:, :, pl.ds(1, 7)], cut_send.at[0])
    landed(right_all.at[pl.ds(1, 7)], cut_send.at[1])
    landed(right_full.at[pl.ds(1, 7)], cut_send.at[2])
    landed(basis_q.at[core, pl.ds(1, 15)], plane_send.at[0])
    landed(basis_s.at[pl.ds(1, 15)], plane_send.at[1])
    landed(right_q.at[core, pl.ds(1, 15)], plane_send.at[2])
    landed(right_s.at[pl.ds(1, 15)], plane_send.at[3])
    for copy in mine + more:
        copy.wait()
    merged_copy.wait()
    swap(0, basis_q).wait()
    swap(1, right_q).wait()


def decompress(member_ref, basis_q, basis_s, right_q, right_s, merged, gradient, new_error,
               bq, bs, rq, rs, mg, ne, out, scale_sem, load_sem, merged_sem, out_sem):
    scales = [pltpu.make_async_copy(basis_s, bs, scale_sem.at[0]),
              pltpu.make_async_copy(right_s, rs, scale_sem.at[1])]
    merges = pltpu.make_async_copy(merged, mg, merged_sem.at[0])
    loads = []
    for g in range(4):
        slots = pl.ds(4 * g, 4)
        loads.append([pltpu.make_async_copy(basis_q.at[:, slots], bq.at[:, slots], load_sem.at[g, 0]),
                      pltpu.make_async_copy(right_q.at[:, slots], rq.at[:, slots], load_sem.at[g, 1])])
    for copy in scales + loads[0] + loads[1] + loads[2] + loads[3] + [merges]:
        copy.start()
    for copy in scales:
        copy.wait()

    def split(values):
        high = values.astype(jnp.bfloat16)
        return high, (values - high.astype(jnp.float32)).astype(jnp.bfloat16)

    zero = jnp.zeros((32, 512), jnp.bfloat16)

    def approx_of(o):
        b = restore(jnp.concatenate([bq[0, o], bq[1, o]], axis=0), bs[o])
        lhs = jnp.concatenate(split(b), axis=1)
        result = []
        for l in range(2):
            r = restore(rq[l, o], rs[o, l])
            high, low = split(jnp.concatenate([r[i] for i in range(4)], axis=1))
            rows = [zero] * 8
            rows[l], rows[l + 2], rows[l + 4], rows[l + 6] = high, low, high, low
            result.append(jnp.dot(lhs, jnp.concatenate(rows, axis=0), preferred_element_type=jnp.float32))
        return result

    writes = []
    for o in range(16):
        if o % 4 == 0:
            for copy in loads[o // 4]:
                copy.wait()
        for l, approx in enumerate(approx_of(o)):
            out[o, l] = approx.astype(jnp.bfloat16)
        j = lax.rem(member_ref[0] - o + 16, 16)
        columns = pl.ds(pl.multiple_of(j * 512, 512), 512)
        writes.append(pltpu.make_async_copy(out.at[o], gradient.at[:, :, columns], out_sem.at[o]))
        writes[-1].start()
    merges.wait()
    for l, approx in enumerate(approx_of(0)):
        ne[l] = mg[l] - approx
    writes.append(pltpu.make_async_copy(ne, new_error, merged_sem.at[1]))
    writes[-1].start()
    for copy in writes:
        copy.wait()


def body(partials, errors, start_seed):
    f32, i16 = jnp.float32, jnp.int16
    vmem = pl.BlockSpec(memory_space=pltpu.VMEM)
    hbm = pl.BlockSpec(memory_space=pl.ANY)
    dma = pltpu.SemaphoreType.DMA
    limit = 60 * 1024 * 1024
    data = [pltpu.VMEM((STEPS, 2, n, *shape, 16, 128), i16) for shape in ((4, 4), (4,)) for n in (2, 4)]
    scales = [pltpu.VMEM((STEPS, 2, 2, n, 1, 128), f32) for n in (4, 2)]
    merged, basis_q, basis_s, right_q, right_s = pl.pallas_call(
        exchange,
        out_shape=(
            jax.ShapeDtypeStruct((2, 256, 512), f32),
            jax.ShapeDtypeStruct((2, 16, 128, 128), i16),
            jax.ShapeDtypeStruct((16, 1, 128), f32),
            jax.ShapeDtypeStruct((2, 16, 4, 32, 128), i16),
            jax.ShapeDtypeStruct((16, 2, 1, 128), f32),
        ),
        in_specs=[hbm, hbm, vmem],
        out_specs=(hbm,) * 5,
        scratch_shapes=[
            pltpu.VMEM((2, 4, 4, 4, 256, 128), f32),
            pltpu.VMEM((2, 256, 512), f32),
            pltpu.VMEM((2, 256, 512), f32),
            pltpu.VMEM((2, 32, 512), f32),
            *data, *data, *scales, *scales,
            pltpu.VMEM((2, 2, 32, 128), f32),
            pltpu.VMEM((2, 2, 8, 32, 128), f32),
            pltpu.VMEM((2, 32, 256), f32),
            pltpu.VMEM((8, 32, 128), f32),
            pltpu.VMEM((8, 32, 128), f32),
            pltpu.VMEM((8, 32, 128), f32),
            pltpu.VMEM((2, 128, 128), i16),
            pltpu.VMEM((2, 4, 32, 128), i16),
            pltpu.VMEM((3, 1, 128), f32),
            dma((3,)),
            dma,
            dma((5,)),
            dma((3, 2)),
            dma((STEPS, 2, 2, 2)),
            dma((3,)),
            dma((3, 2)),
            dma((4,)),
            dma((4,)),
            dma((2, 2)),
        ],
        compiler_params=pltpu.CompilerParams(
            collective_id=0, has_side_effects=True, vmem_limit_bytes=limit),
        name="exchange",
    )(partials.reshape(2, 256, 8192), errors.reshape(2, 256, 512), jnp.swapaxes(start_seed, 1, 2))

    member = lax.axis_index("intra").astype(jnp.int32).reshape(1)
    gradient, new_error = pl.pallas_call(
        decompress,
        out_shape=(
            jax.ShapeDtypeStruct((2, 256, 8192), jnp.bfloat16),
            jax.ShapeDtypeStruct((2, 256, 512), f32),
        ),
        in_specs=[pl.BlockSpec(memory_space=pltpu.SMEM)] + [hbm] * 5,
        out_specs=(hbm, hbm),
        scratch_shapes=[
            pltpu.VMEM((2, 16, 128, 128), i16),
            pltpu.VMEM((16, 1, 128), f32),
            pltpu.VMEM((2, 16, 4, 32, 128), i16),
            pltpu.VMEM((16, 2, 1, 128), f32),
            pltpu.VMEM((2, 256, 512), f32),
            pltpu.VMEM((2, 256, 512), f32),
            pltpu.VMEM((16, 2, 256, 512), jnp.bfloat16),
            dma((2,)),
            dma((4, 2)),
            dma((2,)),
            dma((16,)),
        ],
        compiler_params=pltpu.CompilerParams(vmem_limit_bytes=limit),
        name="decompress",
    )(member, basis_q, basis_s, right_q, right_s, merged)
    return gradient, new_error[None]


def solution(mesh):
    in_specs = (
        P("cuts", "intra", None, None, None),
        P("cuts", None, None, "intra"),
        P(None, "intra", None),
    )
    out_specs = (P(), P("cuts", None, None, "intra"))
    return jax.shard_map(body, mesh=mesh, in_specs=in_specs, out_specs=out_specs, check_vma=False)
```

time: 400 us -> 95.1 us (0.24)
  waiting for transfers between devices: 311 us -> 0 us
  Pallas kernels: 0 us -> 94.4 us
  other arithmetic: 58 us -> 0 us
  between operations: 14 us -> 0.64 us
  local copies, waits for them, and re-layouts: 8.47 us -> 0 us
  matrix products: 6.95 us -> 0 us
    reduce_scatter x1 -> x0, waiting for transfers between devices: 117 us -> none  [body(): lax.psum_scatter(local_part, 'intra', scatter_dimension=2, tiled=True)]
    psum x2 -> x0, waiting for transfers between devices: 115 us -> none  [the longest x1 58.3 us: body(): right = lax.psum(right, 'cuts') / lax.axis_size('cuts')]
    pallas_call x0 -> x2, Pallas kernels: none -> 94.4 us  [the longest x1 88.7 us: body(): pl.pallas_call(exchange, out_shape=(jax.ShapeDtypeStruct((2, 256, 512), f...]
    all_gather x1 -> x0, waiting for transfers between devices: 79 us -> none  [body(): lax.all_gather(approx.astype(jnp.bfloat16), 'intra', axis=2, tiled=True)]
    reduce_sum x91 -> x0, other arithmetic: 32 us -> none  [the longest x59 24.7 us: orthonormal(): jnp.sum(earlier * vector, axis=-1, keepdims=True) * earlier]
    unnamed x31 -> x0, other arithmetic: 24.8 us -> none
    unnamed x7 -> x0, local copies, waits for them, and re-layouts: 7.78 us -> none
    dot_general x3 -> x0, matrix products: 6.95 us -> none  [the longest x1 3.12 us: body(): jnp.einsum('lrk,ldk->lrd', basis, right, precision=lax.Precision.HIGHEST)]
  transfers between devices with their start and end apart: 4 -> 0, of which waited for: 4 -> 0; matrix products, arithmetic and copies ran while one was open for 0% -> 0% of each run, Pallas kernels for 0% -> 0%
where the time goes in v2:
time: 95.1 us; the launch traced here: 95 us
  Pallas kernels  94.4 us (99%)
    pallas_call x1, Pallas kernels, body(): pl.pallas_call(exchange, out_shape=(jax.ShapeDtypeStruct((2, 256, 512), f...  88.7 us
    pallas_call x1, Pallas kernels, body(): pl.pallas_call(decompress, out_shape=(jax.ShapeDtypeStruct((2, 256, 8192)...  5.69 us

profile of v2, /device:TPU:1, one launch (start us, length us, event | category | flops | bytes accessed | tf_op | source)
XLA Modules:
  0.0 95.0 jit_solution(6319989192557709664)
XLA Ops:
  0.6 88.7 %exchange.1 = (f32[2,256,512]{2,1,0:T(8,128)}, s16[2,16,128,128]{3,2,1,0:T(8,128)(2,1)}, f32[16,1,128]{2,1,0:T(1,128)}, s16[2,16,4,32,128]{4,3,2,1,0:T(8,128)(2,1)}, f32[16,2,1,128]{3,2,1,0:T(1,128)}) custom-call(f32[2,256,8192]{2,1,0:T(8,128)} %bitcast.5, f32[2,256,512]{2,1,0:T(8,128)} %bitcast.6, s32[2,32,512]{2,1,0:T(8,128)} %bitcast.7), custom_call_target="tpu_custom_call" | custom-call | tf_op jit(solution)/shard_map/exchange/pallas_call | solution.py:426
  89.3 5.7 %decompress.1 = (bf16[2,256,8192]{2,1,0:T(8,128)(2,1)}, f32[2,256,512]{2,1,0:T(8,128)}) custom-call(s32[1]{0:T(128)} %bitcast.member_ref, s16[2,16,128,128]{3,2,1,0:T(8,128)(2,1)} %get-tuple-element.9.basis_q, f32[16,1,128]{2,1,0:T(1,128)} %get-tuple-element.10.basis_s, s16[2,16,4,32,128]{4,3,2,1,0:T(8,128)(2,1)} %get-tuple-element.11.right_q, ...), custom_call_target="tpu_custom_call" | custom-call | tf_op jit(solution)/shard_map/decompress/pallas_call | solution.py:469

commit v3 on v2

v3 whole, which is shorter than its diff:
```python
import functools

import jax
import jax.numpy as jnp
from jax import lax
from jax.experimental import pallas as pl
from jax.experimental.pallas import tpu as pltpu
from jax.sharding import PartitionSpec as P

MESH = pl.DeviceIdType.MESH
HIGHEST = lax.Precision.HIGHEST
STEPS = 8
LIMIT = 32767.0


def quantize(values):
    top = jnp.abs(values)
    while top.ndim > 2:
        top = jnp.max(top, axis=0)
    top = jnp.maximum(jnp.max(top, axis=0, keepdims=True), 1e-30)
    coded = jnp.round(values * (LIMIT / top)).astype(jnp.int32).astype(jnp.int16)
    return coded, top * (1.0 / LIMIT)


def restore(coded, scale):
    return coded.astype(jnp.int32).astype(jnp.float32) * scale


def exchange(part, errors, seed, merged_out, basis_q, right_q, factor_s,
             own, error_v, merged, mean, start,
             sa1, sb1, sa2, sb2, ra1, rb1, ra2, rb2, ssa, ssb, rsa, rsb,
             shares, left, left_all, vectors, basis, basis_send, right_send, scale_send,
             load_sem, error_sem, out_sem, send_sem, recv_sem, cut_send, cut_recv, left_recv,
             plane_send, plane_recv, swap_sem):
    cut = lax.axis_index("cuts")
    member = lax.axis_index("intra")
    y, z = lax.rem(member, 4), lax.div(member, 4)
    core = lax.rem(cut, 2)

    def wrap(v):
        return lax.rem(v + 8, 4)

    ring = (
        {"plus": (cut, z * 4 + wrap(y + 1)), "minus": (cut, z * 4 + wrap(y - 1)), "pos": y},
        {"plus": (cut, wrap(z + 1) * 4 + y), "minus": (cut, wrap(z - 1) * 4 + y), "pos": z},
    )

    def cut_peer(o):
        return lax.rem(cut + o, 8)

    def plane_peer(o):
        return lax.rem(member + o, 16)

    def load(l, first, count, sem):
        rows = pl.ds(first, count)

        def group(g, _):
            pltpu.make_async_copy(
                part.at[l, rows, pl.ds(pl.multiple_of(g * 128, 128), 128)],
                own.at[l, lax.div(g, 16), lax.rem(lax.div(g, 4), 4), lax.rem(g, 4), rows],
                load_sem.at[sem]).start()
            return 0

        lax.fori_loop(0, 64, group, 0)

    def loaded(l, first, count, sem):
        there = own.at[l, :, :, :, pl.ds(first, count)]
        pltpu.make_async_copy(there, there, load_sem.at[sem]).wait()

    load(0, 0, 64, 0)

    barrier = pltpu.get_barrier_semaphore()
    for o in range(1, 8):
        pl.semaphore_signal(barrier, inc=1, device_id=(cut_peer(o), member), device_id_type=MESH)
    for o in range(1, 16):
        pl.semaphore_signal(barrier, inc=1, device_id=(cut, plane_peer(o)), device_id_type=MESH)

    load(0, 64, 192, 1)
    error_copy = pltpu.make_async_copy(errors, error_v, error_sem)
    error_copy.start()
    load(1, 0, 256, 2)

    for l in range(2):
        start[l] = (seed[l].astype(jnp.float32) - 32760.0) * (1.0 / 18918.0)

    data_send, data_recv = ((sa1, sb1), (sa2, sb2)), ((ra1, rb1), (ra2, rb2))
    scale_slot = ((0, 0), (0, 2), (0, 1), (0, 3), (1, 0), (1, 1))

    def data_copy(t, s, p, m):
        axis = ring[s if p == 0 else 1 - s]
        g, n = (0, m) if m < 2 else (1, m - 2)
        return pltpu.make_async_remote_copy(
            src_ref=data_send[p][g].at[t, s, n], dst_ref=data_recv[p][g].at[t, s, n],
            send_sem=send_sem.at[p, g], recv_sem=recv_sem.at[t, p, g, 0],
            device_id=axis["plus"] if m % 2 == 0 else axis["minus"], device_id_type=MESH)

    def scale_copy(t, s, p, g, side):
        axis = ring[s if p == 0 else 1 - s]
        rows = pl.ds(side * 2, 2) if g == 0 else pl.ds(side, 1)
        there, here = (rsa, ssa) if g == 0 else (rsb, ssb)
        return pltpu.make_async_remote_copy(
            src_ref=here.at[t, p, s, rows], dst_ref=there.at[t, p, s, rows],
            send_sem=send_sem.at[2, g], recv_sem=recv_sem.at[t, p, g, 1],
            device_id=axis["plus"] if side == 0 else axis["minus"], device_id_type=MESH)

    def arrived(t, p, g):
        there = data_recv[p][g].at[t]
        pltpu.make_async_copy(there, there, recv_sem.at[t, p, g, 0]).wait()
        there = (rsa, rsb)[g].at[t, p]
        pltpu.make_async_copy(there, there, recv_sem.at[t, p, g, 1]).wait()

    def rows_of(t, s, h):
        return pl.ds(pl.multiple_of(lax.rem(t, 4) * 64 + s * 32 + h * 16, 16), 16)

    def term(t, s, p, q, h):
        l, rows = lax.div(t, 4), rows_of(t, s, h)
        if p == 0:
            return own[l, :, q, :, rows, :] if s == 0 else own[l, q, :, :, rows, :]
        return own[l, q, y, :, rows, :] if s == 0 else own[l, z, q, :, rows, :]

    def code(t, s, p, m, values):
        coded, scale = quantize(values)
        g, n = (0, m) if m < 2 else (1, m - 2)
        data_send[p][g][t, s, n] = coded
        group, row = scale_slot[m]
        (ssa, ssb)[group][t, p, s, row] = scale

    def got(t, s, p, m):
        g, n = (0, m) if m < 2 else (1, m - 2)
        group, row = scale_slot[m]
        return restore(data_recv[p][g][t, s, n], (rsa, rsb)[group][t, p, s, row])

    def first_code(t, s, p):
        pos = ring[s if p == 0 else 1 - s]["pos"]
        code(t, s, p, 0, term(t, s, p, wrap(pos + 2), 0))
        code(t, s, p, 1, term(t, s, p, wrap(pos + 2), 1))
        code(t, s, p, 2, term(t, s, p, wrap(pos + 1), 1))
        code(t, s, p, 3, term(t, s, p, wrap(pos - 1), 0))

    def first_send(t, s, p):
        for side in range(2):
            scale_copy(t, s, p, 0, side).start()
        for m in range(4):
            data_copy(t, s, p, m).start()

    def second(t, s, p):
        pos = ring[s if p == 0 else 1 - s]["pos"]
        code(t, s, p, 4, term(t, s, p, wrap(pos + 1), 0) + got(t, s, p, 0))
        code(t, s, p, 5, term(t, s, p, wrap(pos - 1), 1) + got(t, s, p, 1))
        for side in range(2):
            scale_copy(t, s, p, 1, side).start()
            data_copy(t, s, p, 4 + side).start()

    def total(t, s, p, h):
        pos = ring[s if p == 0 else 1 - s]["pos"]
        pair = (3, 4) if h == 0 else (2, 5)
        return term(t, s, p, pos, h) + got(t, s, p, pair[0]) + got(t, s, p, pair[1])

    def base_of(u):
        return lax.rem(u, 4) * 64

    def share_copy(u, o):
        rows = pl.ds(pl.multiple_of(base_of(u) + cut_peer(o) * 8, 8), 8)
        return pltpu.make_async_remote_copy(
            src_ref=merged.at[lax.div(u, 4), rows], dst_ref=shares.at[u, o],
            send_sem=cut_send.at[0], recv_sem=cut_recv.at[u, 0],
            device_id=(cut_peer(o), member), device_id_type=MESH)

    def mean_copy(u, o):
        rows = pl.ds(pl.multiple_of(base_of(u) + cut * 8, 8), 8)
        there = mean.at[lax.div(u, 4), rows]
        return pltpu.make_async_remote_copy(
            src_ref=there, dst_ref=there, send_sem=cut_send.at[1], recv_sem=cut_recv.at[u, 1],
            device_id=(cut_peer(o), member), device_id_type=MESH)

    def landed(there, sem):
        pltpu.make_async_copy(there, there, sem).wait()

    def slot(c):
        return lax.rem(cut - c + 8, 8)

    def plane_copy(l, n, o, src, dst):
        return pltpu.make_async_remote_copy(
            src_ref=src, dst_ref=dst, send_sem=plane_send.at[l, n], recv_sem=plane_recv.at[l, n],
            device_id=(cut, plane_peer(o)), device_id_type=MESH)

    def left_copy(l, half, o):
        return pltpu.make_async_remote_copy(
            src_ref=left.at[l, half], dst_ref=left_all.at[l, half, o],
            send_sem=cut_send.at[2], recv_sem=left_recv.at[l, half],
            device_id=(cut_peer(o), member), device_id_type=MESH)

    def own_factors(l):
        return (pltpu.make_async_copy(basis_send.at[l], basis_q.at[l, :, 0], out_sem.at[1, l]),
                pltpu.make_async_copy(right_send.at[l], right_q.at[l, :, 0], out_sem.at[2, l]),
                pltpu.make_async_copy(scale_send.at[l], factor_s.at[l, 0], out_sem.at[3, l]))

    gathered = (basis_q, right_q)

    def swap(l, n):
        there = gathered[n].at[l, core, pl.ds(1, 15)]
        return pltpu.make_async_remote_copy(
            src_ref=there, dst_ref=there, send_sem=swap_sem.at[0, l, n], recv_sem=swap_sem.at[1, l, n],
            device_id=(cut + 1 - 2 * core, member), device_id_type=MESH)

    def pass_on(l, n):
        landed(gathered[n].at[l, core, pl.ds(1, 15)], plane_recv.at[l, n])
        swap(l, n).start()

    def gather_left(l):
        for half in range(2):
            landed(left_all.at[l, half, pl.ds(1, 7)], left_recv.at[l, half])
            summed = left_all[l, half, slot(0)]
            for c in range(1, 8):
                summed = summed + left_all[l, half, slot(c)]
            vectors[:, half * 128:(half + 1) * 128] = summed

    def columns(g):
        later = lax.broadcasted_iota(jnp.int32, (32, 1), 0) - g * 8
        soon = lax.broadcasted_iota(jnp.int32, (8, 1), 0)
        block = vectors[...]
        rows = pl.ds(pl.multiple_of(g * 8, 8), 8)
        group = vectors[rows, :]
        done = []
        for i in range(8):
            v = group[i:i + 1, :]
            size = jnp.sum(v * v, axis=1, keepdims=True) + 1e-6
            done.append(v / jnp.sqrt(size))
            near = jnp.sum(group * v, axis=1, keepdims=True) / size
            group = group - jnp.where(soon > i, near, 0.0) * v
            dots = jnp.sum(block * v, axis=1, keepdims=True) / size
            block = block - jnp.where(later > i, dots, 0.0) * v
        vectors[...] = block
        basis[rows, :] = jnp.concatenate(done, axis=0)

    def send_basis(l):
        coded, scale = quantize(jnp.stack([basis[:, i * 128:(i + 1) * 128] for i in range(2)]))
        basis_send[l] = coded
        scale_send[l, 0] = scale
        for o in range(1, 16):
            plane_copy(l, 0, o, basis_send.at[l, core], basis_q.at[l, core, o]).start()

    def send_right(l):
        right = jnp.dot(basis[...], mean[l], precision=HIGHEST, preferred_element_type=jnp.float32) * 0.125
        coded, scale = quantize(jnp.stack([right[:, i * 128:(i + 1) * 128] for i in range(4)]))
        right_send[l, 0] = coded[:2]
        right_send[l, 1] = coded[2:]
        scale_send[l, 1] = scale
        for o in range(1, 16):
            plane_copy(l, 2, o, scale_send.at[l], factor_s.at[l, o]).start()
            plane_copy(l, 1, o, right_send.at[l, core], right_q.at[l, core, o]).start()
        for copy in own_factors(l):
            copy.start()

    loaded(0, 0, 64, 0)
    for s in range(2):
        first_code(0, s, 0)
    pl.semaphore_wait(barrier, 22)

    def step(t, _):
        @pl.when(t < STEPS)
        def _():
            for s in range(2):
                first_send(t, s, 0)

        @pl.when((t >= 1) & (t < STEPS + 1))
        def _():
            arrived(t - 1, 0, 0)
            for s in range(2):
                second(t - 1, s, 0)

        @pl.when((t >= 2) & (t < STEPS + 2))
        def _():
            u = t - 2
            l = lax.div(u, 4)
            arrived(u, 0, 1)
            for s in range(2):
                for h in range(2):
                    summed = total(u, s, 0, h)
                    if s == 0:
                        own[l, :, y, :, rows_of(u, s, h), :] = summed
                    else:
                        own[l, z, :, :, rows_of(u, s, h), :] = summed
                first_code(u, s, 1)
                first_send(u, s, 1)

        @pl.when((t >= 3) & (t < STEPS + 3))
        def _():
            arrived(t - 3, 1, 0)
            for s in range(2):
                second(t - 3, s, 1)

        @pl.when((t >= 4) & (t < STEPS + 4))
        def _():
            u = t - 4
            l = lax.div(u, 4)
            arrived(u, 1, 1)

            @pl.when(u == 0)
            def _():
                error_copy.wait()

            for s in range(2):
                for h in range(2):
                    rows = rows_of(u, s, h)
                    summed = total(u, s, 1, h)
                    wide = jnp.concatenate([summed[i] for i in range(4)], axis=1)
                    merged[l, rows, :] = wide + error_v[l, rows, :]

            for o in range(1, 8):
                share_copy(u, o).start()

            @pl.when(lax.rem(u, 2) == 1)
            def _():
                half = lax.div(lax.rem(u, 4), 2)
                rows = pl.ds(pl.multiple_of(half * 128, 128), 128)
                left[l, half] = lax.dot_general(
                    start[l], merged[l, rows, :], (((1,), (1,)), ((), ())),
                    precision=HIGHEST, preferred_element_type=jnp.float32)
                for o in range(1, 8):
                    left_copy(l, half, o).start()
                left_all[l, half, 0] = left[l, half]

        @pl.when((t >= 5) & (t < STEPS + 5))
        def _():
            u = t - 5
            l = lax.div(u, 4)
            landed(shares.at[u, pl.ds(1, 7)], cut_recv.at[u, 0])
            rows = pl.ds(pl.multiple_of(base_of(u) + cut * 8, 8), 8)
            shares[u, 0] = merged[l, rows, :]
            summed = shares[u, slot(0)]
            for c in range(1, 8):
                summed = summed + shares[u, slot(c)]
            mean[l, rows, :] = summed
            for o in range(1, 8):
                mean_copy(u, o).start()

        @pl.when(t >= 6)
        def _():
            u = t - 6
            landed(mean.at[lax.div(u, 4), pl.ds(pl.multiple_of(base_of(u), 64), 56)], cut_recv.at[u, 1])

        @pl.when(t == STEPS)
        def _():
            gather_left(0)

        @pl.when((t >= STEPS) & (t < STEPS + 4))
        def _():
            columns(t - STEPS)

        @pl.when(t == STEPS + 3)
        def _():
            send_basis(0)
            send_right(0)

        @pl.when(t == STEPS + 4)
        def _():
            gather_left(1)
            lax.fori_loop(0, 4, lambda g, _: (columns(g), 0)[1], 0)
            send_basis(1)

        @pl.when(t + 1 < STEPS)
        def _():
            @pl.when(t + 1 == 1)
            def _():
                loaded(0, 64, 192, 1)

            @pl.when(t + 1 == 4)
            def _():
                loaded(1, 0, 256, 2)

            for s in range(2):
                first_code(t + 1, s, 0)

        return 0

    lax.fori_loop(0, STEPS + 6, step, 0)

    merged_copy = pltpu.make_async_copy(merged, merged_out, out_sem.at[0, 0])
    merged_copy.start()
    send_right(1)
    for l, n in ((0, 0), (0, 1), (1, 0), (1, 1)):
        pass_on(l, n)

    for p in range(2):
        for g in range(2):
            landed(data_send[p][g], send_sem.at[p, g])
    landed(ssa, send_sem.at[2, 0])
    landed(ssb, send_sem.at[2, 1])
    for n in range(2):
        landed(shares.at[:, pl.ds(1, 7)], cut_send.at[n])
    landed(left_all.at[:, :, pl.ds(1, 7)], cut_send.at[2])
    for l in range(2):
        landed(factor_s.at[l, pl.ds(1, 15)], plane_recv.at[l, 2])
        for n in range(2):
            landed(gathered[n].at[l, core, pl.ds(1, 15)], plane_send.at[l, n])
        landed(factor_s.at[l, pl.ds(1, 15)], plane_send.at[l, 2])
        for copy in own_factors(l):
            copy.wait()
    merged_copy.wait()
    for l in range(2):
        for n in range(2):
            swap(l, n).wait()


def decompress(member_ref, basis_q, right_q, factor_s, merged, gradient, new_error,
               bq, rq, fs, mg, ne, out, scale_sem, load_sem, merged_sem, out_sem):
    scales = pltpu.make_async_copy(factor_s, fs, scale_sem)
    merges = pltpu.make_async_copy(merged, mg, merged_sem.at[0])
    loads = []
    for g in range(4):
        slots = pl.ds(4 * g, 4)
        loads.append(pltpu.make_async_copy(basis_q.at[:, :, slots], bq.at[:, :, slots], load_sem.at[g, 0]))
        loads.append(pltpu.make_async_copy(right_q.at[:, :, slots], rq.at[:, :, slots], load_sem.at[g, 1]))
    for copy in [scales] + loads + [merges]:
        copy.start()
    scales.wait()

    def split(values):
        high = values.astype(jnp.bfloat16)
        return high, (values - high.astype(jnp.float32)).astype(jnp.bfloat16)

    def approx_of(l, o):
        left, right = fs[l, o, 0], fs[l, o, 1]
        b = jnp.concatenate([restore(bq[l, i, o], left) for i in range(2)], axis=1)
        r = jnp.concatenate([restore(rq[l, i // 2, o, i % 2], right) for i in range(4)], axis=1)
        b_high, b_low = split(b)
        r_high, r_low = split(r)
        return lax.dot_general(
            jnp.concatenate([b_high, b_high, b_low], axis=0),
            jnp.concatenate([r_high, r_low, r_high], axis=0),
            (((0,), (0,)), ((), ())), preferred_element_type=jnp.float32)

    writes = []
    for o in range(16):
        if o % 4 == 0:
            loads[o // 2].wait()
            loads[o // 2 + 1].wait()
        for l in range(2):
            out[o, l] = approx_of(l, o).astype(jnp.bfloat16)
        j = lax.rem(member_ref[0] - o + 16, 16)
        columns = pl.ds(pl.multiple_of(j * 512, 512), 512)
        writes.append(pltpu.make_async_copy(out.at[o], gradient.at[:, :, columns], out_sem.at[o]))
        writes[-1].start()
    merges.wait()
    for l in range(2):
        ne[l] = mg[l] - approx_of(l, 0)
    writes.append(pltpu.make_async_copy(ne, new_error, merged_sem.at[1]))
    writes[-1].start()
    for copy in writes:
        copy.wait()


def body(partials, errors, start_seed):
    f32, i16 = jnp.float32, jnp.int16
    vmem = pl.BlockSpec(memory_space=pltpu.VMEM)
    hbm = pl.BlockSpec(memory_space=pl.ANY)
    dma = pltpu.SemaphoreType.DMA
    limit = 60 * 1024 * 1024
    data = [pltpu.VMEM((STEPS, 2, n, *shape, 16, 128), i16) for shape in ((4, 4), (4,)) for n in (2, 4)]
    scales = [pltpu.VMEM((STEPS, 2, 2, n, 1, 128), f32) for n in (4, 2)]
    merged, basis_q, right_q, factor_s = pl.pallas_call(
        exchange,
        out_shape=(
            jax.ShapeDtypeStruct((2, 256, 512), f32),
            jax.ShapeDtypeStruct((2, 2, 16, 32, 128), i16),
            jax.ShapeDtypeStruct((2, 2, 16, 2, 32, 128), i16),
            jax.ShapeDtypeStruct((2, 16, 2, 1, 128), f32),
        ),
        in_specs=[hbm, hbm, vmem],
        out_specs=(hbm,) * 4,
        scratch_shapes=[
            pltpu.VMEM((2, 4, 4, 4, 256, 128), f32),
            pltpu.VMEM((2, 256, 512), f32),
            pltpu.VMEM((2, 256, 512), f32),
            pltpu.VMEM((2, 256, 512), f32),
            pltpu.VMEM((2, 32, 512), f32),
            *data, *data, *scales, *scales,
            pltpu.VMEM((STEPS, 8, 8, 512), f32),
            pltpu.VMEM((2, 2, 32, 128), f32),
            pltpu.VMEM((2, 2, 8, 32, 128), f32),
            pltpu.VMEM((32, 256), f32),
            pltpu.VMEM((32, 256), f32),
            pltpu.VMEM((2, 2, 32, 128), i16),
            pltpu.VMEM((2, 2, 2, 32, 128), i16),
            pltpu.VMEM((2, 2, 1, 128), f32),
            dma((3,)),
            dma,
            dma((4, 2)),
            dma((3, 2)),
            dma((STEPS, 2, 2, 2)),
            dma((3,)),
            dma((STEPS, 2)),
            dma((2, 2)),
            dma((2, 3)),
            dma((2, 3)),
            dma((2, 2, 2)),
        ],
        compiler_params=pltpu.CompilerParams(
            collective_id=0, has_side_effects=True, vmem_limit_bytes=limit),
        name="exchange",
    )(partials.reshape(2, 256, 8192), errors.reshape(2, 256, 512), jnp.swapaxes(start_seed, 1, 2))

    member = lax.axis_index("intra").astype(jnp.int32).reshape(1)
    gradient, new_error = pl.pallas_call(
        decompress,
        out_shape=(
            jax.ShapeDtypeStruct((2, 256, 8192), jnp.bfloat16),
            jax.ShapeDtypeStruct((2, 256, 512), f32),
        ),
        in_specs=[pl.BlockSpec(memory_space=pltpu.SMEM)] + [hbm] * 4,
        out_specs=(hbm, hbm),
        scratch_shapes=[
            pltpu.VMEM((2, 2, 16, 32, 128), i16),
            pltpu.VMEM((2, 2, 16, 2, 32, 128), i16),
            pltpu.VMEM((2, 16, 2, 1, 128), f32),
            pltpu.VMEM((2, 256, 512), f32),
            pltpu.VMEM((2, 256, 512), f32),
            pltpu.VMEM((16, 2, 256, 512), jnp.bfloat16),
            dma,
            dma((4, 2)),
            dma((2,)),
            dma((16,)),
        ],
        compiler_params=pltpu.CompilerParams(vmem_limit_bytes=limit),
        name="decompress",
    )(member, basis_q, right_q, factor_s, merged)
    return gradient, new_error[None]


def solution(mesh):
    in_specs = (
        P("cuts", "intra", None, None, None),
        P("cuts", None, None, "intra"),
        P(None, "intra", None),
    )
    out_specs = (P(), P("cuts", None, None, "intra"))
    return jax.shard_map(body, mesh=mesh, in_specs=in_specs, out_specs=out_specs, check_vma=False)
```

time: 95.1 us -> 89.3 us (0.939)
  Pallas kernels: 94.4 us -> 88.5 us
    pallas_call x1, Pallas kernels: 88.7 us -> 82.8 us  [body(): pl.pallas_call(exchange, out_shape=(jax.ShapeDtypeStruct((2, 256, 512), f...]
where the time goes in v3:
time: 89.3 us; the launch traced here: 89.1 us
  Pallas kernels  88.5 us (99%)
    pallas_call x1, Pallas kernels, body(): pl.pallas_call(exchange, out_shape=(jax.ShapeDtypeStruct((2, 256, 512), f...  82.8 us
    pallas_call x1, Pallas kernels, body(): pl.pallas_call(decompress, out_shape=(jax.ShapeDtypeStruct((2, 256, 8192)...  5.7 us

profile of v3, /device:TPU:1, one launch (start us, length us, event | category | flops | bytes accessed | tf_op | source)
XLA Modules:
  0.0 89.1 jit_solution(961078917556018755)
XLA Ops:
  0.6 82.8 %exchange.1 = (f32[2,256,512]{2,1,0:T(8,128)}, s16[2,2,16,32,128]{4,3,2,1,0:T(8,128)(2,1)}, s16[2,2,16,2,32,128]{5,4,3,2,1,0:T(8,128)(2,1)}, f32[2,16,2,1,128]{4,3,2,1,0:T(1,128)}) custom-call(f32[2,256,8192]{2,1,0:T(8,128)} %bitcast.5, f32[2,256,512]{2,1,0:T(8,128)} %bitcast.6, s32[2,32,512]{2,1,0:T(8,128)} %bitcast.7), custom_call_target="tpu_custom_call" | custom-call | tf_op jit(solution)/shard_map/exchange/pallas_call | solution.py:462
  83.4 5.7 %decompress.1 = (bf16[2,256,8192]{2,1,0:T(8,128)(2,1)}, f32[2,256,512]{2,1,0:T(8,128)}) custom-call(s32[1]{0:T(128)} %bitcast.member_ref, s16[2,2,16,32,128]{4,3,2,1,0:T(8,128)(2,1)} %get-tuple-element.8.basis_q, s16[2,2,16,2,32,128]{5,4,3,2,1,0:T(8,128)(2,1)} %get-tuple-element.9.right_q, f32[2,16,2,1,128]{4,3,2,1,0:T(1,128)} %get-tuple-element.10.factor_s, ...), custom_call_target="tpu_custom_call" | custom-call | tf_op jit(solution)/shard_map/decompress/pallas_call | solution.py:505

commit v4 on v3

--- a/solution.py
+++ b/solution.py
@@ -31,7 +31,7 @@
              sa1, sb1, sa2, sb2, ra1, rb1, ra2, rb2, ssa, ssb, rsa, rsb,
              shares, left, left_all, vectors, basis, basis_send, right_send, scale_send,
              load_sem, error_sem, out_sem, send_sem, recv_sem, cut_send, cut_recv, left_recv,
-             plane_send, plane_recv, swap_sem):
+             plane_send, plane_recv, swap_sem, ready):
     cut = lax.axis_index("cuts")
     member = lax.axis_index("intra")
     y, z = lax.rem(member, 4), lax.div(member, 4)
@@ -70,10 +70,9 @@
     load(0, 0, 64, 0)
 
     barrier = pltpu.get_barrier_semaphore()
-    for o in range(1, 8):
-        pl.semaphore_signal(barrier, inc=1, device_id=(cut_peer(o), member), device_id_type=MESH)
-    for o in range(1, 16):
-        pl.semaphore_signal(barrier, inc=1, device_id=(cut, plane_peer(o)), device_id_type=MESH)
+    x_side = [(cut_peer(2), member), (cut_peer(6), member), (cut + 1 - 2 * core, member)]
+    for there in x_side + [ring[s][side] for s in range(2) for side in ("plus", "minus")]:
+        pl.semaphore_signal(barrier, inc=1, device_id=there, device_id_type=MESH)
 
     load(0, 64, 192, 1)
     error_copy = pltpu.make_async_copy(errors, error_v, error_sem)
@@ -255,13 +254,28 @@
     loaded(0, 0, 64, 0)
     for s in range(2):
         first_code(0, s, 0)
-    pl.semaphore_wait(barrier, 22)
+    pl.semaphore_wait(barrier, 7)
+
+    def tell(n):
+        for there in x_side:
+            pl.semaphore_signal(ready.at[n], inc=1, device_id=there, device_id_type=MESH)
+
+    tell(0)
 
     def step(t, _):
         @pl.when(t < STEPS)
         def _():
             for s in range(2):
                 first_send(t, s, 0)
+
+        @pl.when(t == 1)
+        def _():
+            pl.semaphore_wait(ready.at[0], 3)
+            tell(1)
+
+        @pl.when(t == 3)
+        def _():
+            pl.semaphore_wait(ready.at[1], 3)
 
         @pl.when((t >= 1) & (t < STEPS + 1))
         def _():
@@ -495,6 +509,7 @@
             dma((2, 3)),
             dma((2, 3)),
             dma((2, 2, 2)),
+            pltpu.SemaphoreType.REGULAR((2,)),
         ],
         compiler_params=pltpu.CompilerParams(
             collective_id=0, has_side_effects=True, vmem_limit_bytes=limit),

time: 89.3 us -> 88 us (0.985)
  Pallas kernels: 88.5 us -> 87.2 us
    pallas_call x1, Pallas kernels: 82.8 us -> 81.5 us  [body(): pl.pallas_call(exchange, out_shape=(jax.ShapeDtypeStruct((2, 256, 512), f...]
where the time goes in v4:
time: 88 us; the launch traced here: 87.8 us
  Pallas kernels  87.2 us (99%)
    pallas_call x1, Pallas kernels, body(): pl.pallas_call(exchange, out_shape=(jax.ShapeDtypeStruct((2, 256, 512), f...  81.5 us
    pallas_call x1, Pallas kernels, body(): pl.pallas_call(decompress, out_shape=(jax.ShapeDtypeStruct((2, 256, 8192)...  5.7 us

profile of v4, /device:TPU:1, one launch (start us, length us, event | category | flops | bytes accessed | tf_op | source)
XLA Modules:
  0.0 87.8 jit_solution(9932404656180951957)
XLA Ops:
  0.6 81.5 %exchange.1 = (f32[2,256,512]{2,1,0:T(8,128)}, s16[2,2,16,32,128]{4,3,2,1,0:T(8,128)(2,1)}, s16[2,2,16,2,32,128]{5,4,3,2,1,0:T(8,128)(2,1)}, f32[2,16,2,1,128]{4,3,2,1,0:T(1,128)}) custom-call(f32[2,256,8192]{2,1,0:T(8,128)} %bitcast.5, f32[2,256,512]{2,1,0:T(8,128)} %bitcast.6, s32[2,32,512]{2,1,0:T(8,128)} %bitcast.7), custom_call_target="tpu_custom_call" | custom-call | tf_op jit(solution)/shard_map/exchange/pallas_call | solution.py:476
  82.1 5.7 %decompress.1 = (bf16[2,256,8192]{2,1,0:T(8,128)(2,1)}, f32[2,256,512]{2,1,0:T(8,128)}) custom-call(s32[1]{0:T(128)} %bitcast.member_ref, s16[2,2,16,32,128]{4,3,2,1,0:T(8,128)(2,1)} %get-tuple-element.8.basis_q, s16[2,2,16,2,32,128]{5,4,3,2,1,0:T(8,128)(2,1)} %get-tuple-element.9.right_q, f32[2,16,2,1,128]{4,3,2,1,0:T(1,128)} %get-tuple-element.10.factor_s, ...), custom_call_target="tpu_custom_call" | custom-call | tf_op jit(solution)/shard_map/decompress/pallas_call | solution.py:520

commit v5 on v4

--- a/solution.py
+++ b/solution.py
@@ -29,7 +29,7 @@
 def exchange(part, errors, seed, merged_out, basis_q, right_q, factor_s,
              own, error_v, merged, mean, start,
              sa1, sb1, sa2, sb2, ra1, rb1, ra2, rb2, ssa, ssb, rsa, rsb,
-             shares, left, left_all, vectors, basis, basis_send, right_send, scale_send,
+             share_send, share_recv, mean_coded, share_scale, share_rscale, mean_scale, left, left_all, vectors, basis, basis_send, right_send, scale_send,
              load_sem, error_sem, out_sem, send_sem, recv_sem, cut_send, cut_recv, left_recv,
              plane_send, plane_recv, swap_sem, ready):
     cut = lax.axis_index("cuts")
@@ -41,8 +41,10 @@
         return lax.rem(v + 8, 4)
 
     ring = (
-        {"plus": (cut, z * 4 + wrap(y + 1)), "minus": (cut, z * 4 + wrap(y - 1)), "pos": y},
-        {"plus": (cut, wrap(z + 1) * 4 + y), "minus": (cut, wrap(z - 1) * 4 + y), "pos": z},
+        {"plus": (cut, z * 4 + wrap(y + 1)), "minus": (cut, z * 4 + wrap(y - 1)),
+         "far": (cut, z * 4 + wrap(y + 2)), "pos": y},
+        {"plus": (cut, wrap(z + 1) * 4 + y), "minus": (cut, wrap(z - 1) * 4 + y),
+         "far": (cut, wrap(z + 2) * 4 + y), "pos": z},
     )
 
     def cut_peer(o):
@@ -85,13 +87,14 @@
     data_send, data_recv = ((sa1, sb1), (sa2, sb2)), ((ra1, rb1), (ra2, rb2))
     scale_slot = ((0, 0), (0, 2), (0, 1), (0, 3), (1, 0), (1, 1))
 
-    def data_copy(t, s, p, m):
+    def data_copy(t, s, p, m, direct=False):
         axis = ring[s if p == 0 else 1 - s]
+        to = axis["far"] if direct and m < 2 else axis["plus"] if m % 2 == 0 else axis["minus"]
         g, n = (0, m) if m < 2 else (1, m - 2)
         return pltpu.make_async_remote_copy(
             src_ref=data_send[p][g].at[t, s, n], dst_ref=data_recv[p][g].at[t, s, n],
             send_sem=send_sem.at[p, g], recv_sem=recv_sem.at[t, p, g, 0],
-            device_id=axis["plus"] if m % 2 == 0 else axis["minus"], device_id_type=MESH)
+            device_id=to, device_id_type=MESH)
 
     def scale_copy(t, s, p, g, side):
         axis = ring[s if p == 0 else 1 - s]
@@ -102,17 +105,33 @@
             send_sem=send_sem.at[2, g], recv_sem=recv_sem.at[t, p, g, 1],
             device_id=axis["plus"] if side == 0 else axis["minus"], device_id_type=MESH)
 
+    def direct_scale_copy(t, s, p, row):
+        axis = ring[s if p == 0 else 1 - s]
+        return pltpu.make_async_remote_copy(
+            src_ref=ssa.at[t, p, s, pl.ds(row, 1)], dst_ref=rsa.at[t, p, s, pl.ds(row, 1)],
+            send_sem=send_sem.at[2, 0], recv_sem=recv_sem.at[t, p, 0, 1],
+            device_id=(axis["far"], axis["plus"], axis["far"], axis["minus"])[row], device_id_type=MESH)
+
     def arrived(t, p, g):
         there = data_recv[p][g].at[t]
         pltpu.make_async_copy(there, there, recv_sem.at[t, p, g, 0]).wait()
         there = (rsa, rsb)[g].at[t, p]
         pltpu.make_async_copy(there, there, recv_sem.at[t, p, g, 1]).wait()
 
+    def div4(t):
+        return t // 4 if isinstance(t, int) else lax.div(t, 4)
+
+    def rem4(t):
+        return t % 4 if isinstance(t, int) else lax.rem(t, 4)
+
+    def at(first, size, unit):
+        return pl.ds(first if isinstance(first, int) else pl.multiple_of(first, unit), size)
+
     def rows_of(t, s, h):
-        return pl.ds(pl.multiple_of(lax.rem(t, 4) * 64 + s * 32 + h * 16, 16), 16)
+        return at(rem4(t) * 64 + s * 32 + h * 16, 16, 16)
 
     def term(t, s, p, q, h):
-        l, rows = lax.div(t, 4), rows_of(t, s, h)
+        l, rows = div4(t), rows_of(t, s, h)
         if p == 0:
             return own[l, :, q, :, rows, :] if s == 0 else own[l, q, :, :, rows, :]
         return own[l, q, y, :, rows, :] if s == 0 else own[l, z, q, :, rows, :]
@@ -141,6 +160,20 @@
             scale_copy(t, s, p, 0, side).start()
         for m in range(4):
             data_copy(t, s, p, m).start()
+
+    def direct_code(t, s, p):
+        pos = ring[s if p == 0 else 1 - s]["pos"]
+        first_code(t, s, p)
+        code(t, s, p, 4, term(t, s, p, wrap(pos + 1), 0))
+        code(t, s, p, 5, term(t, s, p, wrap(pos - 1), 1))
+
+    def direct_send(t, s, p):
+        for row in range(4):
+            direct_scale_copy(t, s, p, row).start()
+        for side in range(2):
+            scale_copy(t, s, p, 1, side).start()
+        for m in range(6):
+            data_copy(t, s, p, m, True).start()
 
     def second(t, s, p):
         pos = ring[s if p == 0 else 1 - s]["pos"]
@@ -150,27 +183,38 @@
             scale_copy(t, s, p, 1, side).start()
             data_copy(t, s, p, 4 + side).start()
 
-    def total(t, s, p, h):
+    def total(t, s, p, h, direct=False):
         pos = ring[s if p == 0 else 1 - s]["pos"]
         pair = (3, 4) if h == 0 else (2, 5)
-        return term(t, s, p, pos, h) + got(t, s, p, pair[0]) + got(t, s, p, pair[1])
+        summed = term(t, s, p, pos, h) + got(t, s, p, pair[0]) + got(t, s, p, pair[1])
+        return summed + got(t, s, p, h) if direct else summed
 
     def base_of(u):
-        return lax.rem(u, 4) * 64
-
-    def share_copy(u, o):
-        rows = pl.ds(pl.multiple_of(base_of(u) + cut_peer(o) * 8, 8), 8)
-        return pltpu.make_async_remote_copy(
-            src_ref=merged.at[lax.div(u, 4), rows], dst_ref=shares.at[u, o],
-            send_sem=cut_send.at[0], recv_sem=cut_recv.at[u, 0],
+        return rem4(u) * 64
+
+    def share_copies(u, o):
+        return [pltpu.make_async_remote_copy(
+            src_ref=src.at[u, cut_peer(o)], dst_ref=dst.at[u, o],
+            send_sem=cut_send.at[n], recv_sem=cut_recv.at[u, n],
             device_id=(cut_peer(o), member), device_id_type=MESH)
-
-    def mean_copy(u, o):
-        rows = pl.ds(pl.multiple_of(base_of(u) + cut * 8, 8), 8)
-        there = mean.at[lax.div(u, 4), rows]
-        return pltpu.make_async_remote_copy(
-            src_ref=there, dst_ref=there, send_sem=cut_send.at[1], recv_sem=cut_recv.at[u, 1],
+            for n, (src, dst) in enumerate(((share_send, share_recv), (share_scale, share_rscale)))]
+
+    def mean_copies(u, o):
+        return [pltpu.make_async_remote_copy(
+            src_ref=ref.at[u, cut], dst_ref=ref.at[u, cut],
+            send_sem=cut_send.at[2 + n], recv_sem=cut_recv.at[u, 2 + n],
             device_id=(cut_peer(o), member), device_id_type=MESH)
+            for n, ref in enumerate((mean_coded, mean_scale))]
+
+    def fold(rows):
+        slices = rows.reshape(8, 8, 512)
+        columns = [slices[:, :, i * 128:(i + 1) * 128] for i in range(4)]
+        pairs = [jnp.concatenate(columns[i:i + 2], axis=1) for i in (0, 2)]
+        return jnp.stack(pairs, axis=1)
+
+    def unfold(slices):
+        columns = [slices[:, i // 2, (i % 2) * 8:(i % 2) * 8 + 8] for i in range(4)]
+        return jnp.concatenate(columns, axis=2).reshape(64, 512)
 
     def landed(there, sem):
         pltpu.make_async_copy(there, there, sem).wait()
@@ -186,7 +230,7 @@
     def left_copy(l, half, o):
         return pltpu.make_async_remote_copy(
             src_ref=left.at[l, half], dst_ref=left_all.at[l, half, o],
-            send_sem=cut_send.at[2], recv_sem=left_recv.at[l, half],
+            send_sem=cut_send.at[4], recv_sem=left_recv.at[l, half],
             device_id=(cut_peer(o), member), device_id_type=MESH)
 
     def own_factors(l):
@@ -218,7 +262,7 @@
         later = lax.broadcasted_iota(jnp.int32, (32, 1), 0) - g * 8
         soon = lax.broadcasted_iota(jnp.int32, (8, 1), 0)
         block = vectors[...]
-        rows = pl.ds(pl.multiple_of(g * 8, 8), 8)
+        rows = at(g * 8, 8, 8)
         group = vectors[rows, :]
         done = []
         for i in range(8):
@@ -262,11 +306,80 @@
 
     tell(0)
 
+    def stage1(u):
+        arrived(u, 0, 0)
+        for s in range(2):
+            second(u, s, 0)
+
+    def stage2(u, direct=False, onward=False):
+        l = div4(u)
+        if direct:
+            arrived(u, 0, 0)
+        arrived(u, 0, 1)
+        for s in range(2):
+            for h in range(2):
+                summed = total(u, s, 0, h, direct)
+                if s == 0:
+                    own[l, :, y, :, rows_of(u, s, h), :] = summed
+                else:
+                    own[l, z, :, :, rows_of(u, s, h), :] = summed
+            (direct_code if onward else first_code)(u, s, 1)
+            (direct_send if onward else first_send)(u, s, 1)
+
+    def stage3(u):
+        arrived(u, 1, 0)
+        for s in range(2):
+            second(u, s, 1)
+
+    def stage4(u, direct=False):
+        l = div4(u)
+        if direct:
+            arrived(u, 1, 0)
+        arrived(u, 1, 1)
+        for s in range(2):
+            for h in range(2):
+                rows = rows_of(u, s, h)
+                summed = total(u, s, 1, h, direct)
+                wide = jnp.concatenate([summed[i] for i in range(4)], axis=1)
+                merged[l, rows, :] = wide + error_v[l, rows, :]
+        folded = fold(merged[l, at(base_of(u), 64, 64), :])
+        top = jnp.max(jnp.max(jnp.abs(folded), axis=1, keepdims=True), axis=2, keepdims=True)
+        top = jnp.maximum(top, 1e-30)
+        share_send[u] = jnp.round(folded * (LIMIT / top)).astype(jnp.int32).astype(jnp.int16)
+        share_scale[u] = top[:, 0] * (1.0 / LIMIT)
+        for o in range(1, 8):
+            for copy in share_copies(u, o):
+                copy.start()
+
+    def send_left(l, half):
+        left[l, half] = lax.dot_general(
+            start[l], merged[l, pl.ds(half * 128, 128), :], (((1,), (1,)), ((), ())),
+            precision=HIGHEST, preferred_element_type=jnp.float32)
+        for o in range(1, 8):
+            left_copy(l, half, o).start()
+        left_all[l, half, 0] = left[l, half]
+
+    def stage5(u):
+        landed(share_recv.at[u, pl.ds(1, 7)], cut_recv.at[u, 0])
+        landed(share_rscale.at[u, pl.ds(1, 7)], cut_recv.at[u, 1])
+        summed = restore(share_send[u, cut], share_scale[u, cut])
+        for o in range(1, 8):
+            summed = summed + restore(share_recv[u, o], share_rscale[u, o])
+        coded, scale = quantize(summed)
+        mean_coded[u, cut] = coded
+        mean_scale[u, cut] = scale
+        for o in range(1, 8):
+            for copy in mean_copies(u, o):
+                copy.start()
+
+    def stage6(u):
+        landed(mean_coded.at[u, pl.ds(0, 7)], cut_recv.at[u, 2])
+        landed(mean_scale.at[u, pl.ds(0, 7)], cut_recv.at[u, 3])
+        mean[div4(u), at(base_of(u), 64, 64), :] = unfold(restore(mean_coded[u], mean_scale[u][:, None]))
+
     def step(t, _):
-        @pl.when(t < STEPS)
-        def _():
-            for s in range(2):
-                first_send(t, s, 0)
+        for s in range(2):
+            first_send(t, s, 0)
 
         @pl.when(t == 1)
         def _():
@@ -277,103 +390,17 @@
         def _():
             pl.semaphore_wait(ready.at[1], 3)
 
-        @pl.when((t >= 1) & (t < STEPS + 1))
-        def _():
-            arrived(t - 1, 0, 0)
-            for s in range(2):
-                second(t - 1, s, 0)
-
-        @pl.when((t >= 2) & (t < STEPS + 2))
-        def _():
-            u = t - 2
-            l = lax.div(u, 4)
-            arrived(u, 0, 1)
-            for s in range(2):
-                for h in range(2):
-                    summed = total(u, s, 0, h)
-                    if s == 0:
-                        own[l, :, y, :, rows_of(u, s, h), :] = summed
-                    else:
-                        own[l, z, :, :, rows_of(u, s, h), :] = summed
-                first_code(u, s, 1)
-                first_send(u, s, 1)
-
-        @pl.when((t >= 3) & (t < STEPS + 3))
-        def _():
-            arrived(t - 3, 1, 0)
-            for s in range(2):
-                second(t - 3, s, 1)
-
-        @pl.when((t >= 4) & (t < STEPS + 4))
-        def _():
-            u = t - 4
-            l = lax.div(u, 4)
-            arrived(u, 1, 1)
-
-            @pl.when(u == 0)
+        for lag, stage in ((1, stage1), (2, stage2), (3, stage3), (4, stage4)):
+            @pl.when(t >= lag)
             def _():
-                error_copy.wait()
-
-            for s in range(2):
-                for h in range(2):
-                    rows = rows_of(u, s, h)
-                    summed = total(u, s, 1, h)
-                    wide = jnp.concatenate([summed[i] for i in range(4)], axis=1)
-                    merged[l, rows, :] = wide + error_v[l, rows, :]
-
-            for o in range(1, 8):
-                share_copy(u, o).start()
-
-            @pl.when(lax.rem(u, 2) == 1)
-            def _():
-                half = lax.div(lax.rem(u, 4), 2)
-                rows = pl.ds(pl.multiple_of(half * 128, 128), 128)
-                left[l, half] = lax.dot_general(
-                    start[l], merged[l, rows, :], (((1,), (1,)), ((), ())),
-                    precision=HIGHEST, preferred_element_type=jnp.float32)
-                for o in range(1, 8):
-                    left_copy(l, half, o).start()
-                left_all[l, half, 0] = left[l, half]
-
-        @pl.when((t >= 5) & (t < STEPS + 5))
-        def _():
-            u = t - 5
-            l = lax.div(u, 4)
-            landed(shares.at[u, pl.ds(1, 7)], cut_recv.at[u, 0])
-            rows = pl.ds(pl.multiple_of(base_of(u) + cut * 8, 8), 8)
-            shares[u, 0] = merged[l, rows, :]
-            summed = shares[u, slot(0)]
-            for c in range(1, 8):
-                summed = summed + shares[u, slot(c)]
-            mean[l, rows, :] = summed
-            for o in range(1, 8):
-                mean_copy(u, o).start()
-
-        @pl.when(t >= 6)
-        def _():
-            u = t - 6
-            landed(mean.at[lax.div(u, 4), pl.ds(pl.multiple_of(base_of(u), 64), 56)], cut_recv.at[u, 1])
-
-        @pl.when(t == STEPS)
-        def _():
-            gather_left(0)
-
-        @pl.when((t >= STEPS) & (t < STEPS + 4))
-        def _():
-            columns(t - STEPS)
-
-        @pl.when(t == STEPS + 3)
-        def _():
-            send_basis(0)
-            send_right(0)
-
-        @pl.when(t == STEPS + 4)
-        def _():
-            gather_left(1)
-            lax.fori_loop(0, 4, lambda g, _: (columns(g), 0)[1], 0)
-            send_basis(1)
-
-        @pl.when(t + 1 < STEPS)
+                if lag == 4:
+                    @pl.when(t == 4)
+                    def _():
+                        error_copy.wait()
+
+                stage(t - lag)
+
+        @pl.when(t + 1 < 6)
         def _():
             @pl.when(t + 1 == 1)
             def _():
@@ -388,7 +415,50 @@
 
         return 0
 
-    lax.fori_loop(0, STEPS + 6, step, 0)
+    lax.fori_loop(0, 6, step, 0)
+    stage5(0)
+    for u in (6, 7):
+        for s in range(2):
+            (direct_code if u == 7 else first_code)(u, s, 0)
+            (direct_send if u == 7 else first_send)(u, s, 0)
+        stage1(u - 1)
+        stage2(u - 2)
+        stage3(u - 3)
+        stage4(u - 4)
+        send_left(0, u - 6)
+        stage5(u - 5)
+        stage6(u - 6)
+
+    stage2(7, True, True)
+    stage2(6, False, True)
+    stage3(5)
+    stage4(4)
+    stage5(3)
+    stage6(2)
+    gather_left(0)
+    columns(0)
+    columns(1)
+
+    stage4(7, True)
+    stage4(6, True)
+    stage4(5)
+    send_left(1, 1)
+    send_left(1, 0)
+    stage5(4)
+    stage6(3)
+    columns(2)
+    columns(3)
+    send_basis(0)
+    send_right(0)
+
+    for u in (7, 6, 5):
+        stage5(u)
+    stage6(4)
+    gather_left(1)
+    lax.fori_loop(0, 4, lambda g, _: (columns(g), 0)[1], 0)
+    send_basis(1)
+    for u in (5, 6, 7):
+        stage6(u)
 
     merged_copy = pltpu.make_async_copy(merged, merged_out, out_sem.at[0, 0])
     merged_copy.start()
@@ -401,9 +471,9 @@
             landed(data_send[p][g], send_sem.at[p, g])
     landed(ssa, send_sem.at[2, 0])
     landed(ssb, send_sem.at[2, 1])
-    for n in range(2):
-        landed(shares.at[:, pl.ds(1, 7)], cut_send.at[n])
-    landed(left_all.at[:, :, pl.ds(1, 7)], cut_send.at[2])
+    for n, ref in enumerate((share_recv, share_rscale, share_recv, share_rscale)):
+        landed(ref.at[:, pl.ds(1, 7)], cut_send.at[n])
+    landed(left_all.at[:, :, pl.ds(1, 7)], cut_send.at[4])
     for l in range(2):
         landed(factor_s.at[l, pl.ds(1, 15)], plane_recv.at[l, 2])
         for n in range(2):
@@ -490,7 +560,8 @@
             pltpu.VMEM((2, 256, 512), f32),
             pltpu.VMEM((2, 32, 512), f32),
             *data, *data, *scales, *scales,
-            pltpu.VMEM((STEPS, 8, 8, 512), f32),
+            *[pltpu.VMEM((STEPS, 8, 2, 16, 128), i16)] * 3,
+            *[pltpu.VMEM((STEPS, 8, 1, 128), f32)] * 3,
             pltpu.VMEM((2, 2, 32, 128), f32),
             pltpu.VMEM((2, 2, 8, 32, 128), f32),
             pltpu.VMEM((32, 256), f32),
@@ -503,8 +574,8 @@
             dma((4, 2)),
             dma((3, 2)),
             dma((STEPS, 2, 2, 2)),
-            dma((3,)),
-            dma((STEPS, 2)),
+            dma((5,)),
+            dma((STEPS, 4)),
             dma((2, 2)),
             dma((2, 3)),
             dma((2, 3)),

time: 88 us -> 85.2 us (0.968)
  Pallas kernels: 87.2 us -> 84.2 us
    pallas_call x1, Pallas kernels: 81.5 us -> 78.5 us  [body(): pl.pallas_call(exchange, out_shape=(jax.ShapeDtypeStruct((2, 256, 512), f...]
where the time goes in v5:
time: 85.2 us; the launch traced here: 85 us
  Pallas kernels  84.2 us (99%)
    pallas_call x1, Pallas kernels, body(): pl.pallas_call(exchange, out_shape=(jax.ShapeDtypeStruct((2, 256, 512), f...  78.5 us
    pallas_call x1, Pallas kernels, body(): pl.pallas_call(decompress, out_shape=(jax.ShapeDtypeStruct((2, 256, 8192)...  5.71 us

profile of v5, /device:TPU:1, one launch (start us, length us, event | category | flops | bytes accessed | tf_op | source)
XLA Modules:
  0.0 85.0 jit_solution(3949929353775729289)
XLA Ops:
  0.6 78.5 %exchange.1 = (f32[2,256,512]{2,1,0:T(8,128)}, s16[2,2,16,32,128]{4,3,2,1,0:T(8,128)(2,1)}, s16[2,2,16,2,32,128]{5,4,3,2,1,0:T(8,128)(2,1)}, f32[2,16,2,1,128]{4,3,2,1,0:T(1,128)}) custom-call(f32[2,256,8192]{2,1,0:T(8,128)} %bitcast.5, f32[2,256,512]{2,1,0:T(8,128)} %bitcast.6, s32[2,32,512]{2,1,0:T(8,128)} %bitcast.7), custom_call_target="tpu_custom_call" | custom-call | tf_op jit(solution)/shard_map/exchange/pallas_call | solution.py:546
  79.2 5.7 %decompress.1 = (bf16[2,256,8192]{2,1,0:T(8,128)(2,1)}, f32[2,256,512]{2,1,0:T(8,128)}) custom-call(s32[1]{0:T(128)} %bitcast.member_ref, s16[2,2,16,32,128]{4,3,2,1,0:T(8,128)(2,1)} %get-tuple-element.8.basis_q, s16[2,2,16,2,32,128]{5,4,3,2,1,0:T(8,128)(2,1)} %get-tuple-element.9.right_q, f32[2,16,2,1,128]{4,3,2,1,0:T(1,128)} %get-tuple-element.10.factor_s, ...), custom_call_target="tpu_custom_call" | custom-call | tf_op jit(solution)/shard_map/decompress/pallas_call | solution.py:591

commit v6 on v5

--- a/solution.py
+++ b/solution.py
@@ -31,7 +31,7 @@
              sa1, sb1, sa2, sb2, ra1, rb1, ra2, rb2, ssa, ssb, rsa, rsb,
              share_send, share_recv, mean_coded, share_scale, share_rscale, mean_scale, left, left_all, vectors, basis, basis_send, right_send, scale_send,
              load_sem, error_sem, out_sem, send_sem, recv_sem, cut_send, cut_recv, left_recv,
-             plane_send, plane_recv, swap_sem, ready):
+             plane_send, plane_recv, swap_sem, ready, measure):
     cut = lax.axis_index("cuts")
     member = lax.axis_index("intra")
     y, z = lax.rem(member, 4), lax.div(member, 4)
@@ -93,7 +93,7 @@
         g, n = (0, m) if m < 2 else (1, m - 2)
         return pltpu.make_async_remote_copy(
             src_ref=data_send[p][g].at[t, s, n], dst_ref=data_recv[p][g].at[t, s, n],
-            send_sem=send_sem.at[p, g], recv_sem=recv_sem.at[t, p, g, 0],
+            send_sem=send_sem.at[p, g], recv_sem=recv_sem.at[t, p, g],
             device_id=to, device_id_type=MESH)
 
     def scale_copy(t, s, p, g, side):
@@ -102,21 +102,21 @@
         there, here = (rsa, ssa) if g == 0 else (rsb, ssb)
         return pltpu.make_async_remote_copy(
             src_ref=here.at[t, p, s, rows], dst_ref=there.at[t, p, s, rows],
-            send_sem=send_sem.at[2, g], recv_sem=recv_sem.at[t, p, g, 1],
+            send_sem=send_sem.at[2, g], recv_sem=recv_sem.at[t, p, g],
             device_id=axis["plus"] if side == 0 else axis["minus"], device_id_type=MESH)
 
     def direct_scale_copy(t, s, p, row):
         axis = ring[s if p == 0 else 1 - s]
         return pltpu.make_async_remote_copy(
             src_ref=ssa.at[t, p, s, pl.ds(row, 1)], dst_ref=rsa.at[t, p, s, pl.ds(row, 1)],
-            send_sem=send_sem.at[2, 0], recv_sem=recv_sem.at[t, p, 0, 1],
+            send_sem=send_sem.at[2, 0], recv_sem=recv_sem.at[t, p, 0],
             device_id=(axis["far"], axis["plus"], axis["far"], axis["minus"])[row], device_id_type=MESH)
 
+    def count(rows, sem):
+        pltpu.make_async_copy(measure.at[pl.ds(0, rows)], measure.at[pl.ds(0, rows)], sem).wait()
+
     def arrived(t, p, g):
-        there = data_recv[p][g].at[t]
-        pltpu.make_async_copy(there, there, recv_sem.at[t, p, g, 0]).wait()
-        there = (rsa, rsb)[g].at[t, p]
-        pltpu.make_async_copy(there, there, recv_sem.at[t, p, g, 1]).wait()
+        count(((520, 1028), (136, 260))[p][g], recv_sem.at[t, p, g])
 
     def div4(t):
         return t // 4 if isinstance(t, int) else lax.div(t, 4)
@@ -195,14 +195,14 @@
     def share_copies(u, o):
         return [pltpu.make_async_remote_copy(
             src_ref=src.at[u, cut_peer(o)], dst_ref=dst.at[u, o],
-            send_sem=cut_send.at[n], recv_sem=cut_recv.at[u, n],
+            send_sem=cut_send.at[n], recv_sem=cut_recv.at[u, 0],
             device_id=(cut_peer(o), member), device_id_type=MESH)
             for n, (src, dst) in enumerate(((share_send, share_recv), (share_scale, share_rscale)))]
 
     def mean_copies(u, o):
         return [pltpu.make_async_remote_copy(
             src_ref=ref.at[u, cut], dst_ref=ref.at[u, cut],
-            send_sem=cut_send.at[2 + n], recv_sem=cut_recv.at[u, 2 + n],
+            send_sem=cut_send.at[2 + n], recv_sem=cut_recv.at[u, 1],
             device_id=(cut_peer(o), member), device_id_type=MESH)
             for n, ref in enumerate((mean_coded, mean_scale))]
 
@@ -360,8 +360,7 @@
         left_all[l, half, 0] = left[l, half]
 
     def stage5(u):
-        landed(share_recv.at[u, pl.ds(1, 7)], cut_recv.at[u, 0])
-        landed(share_rscale.at[u, pl.ds(1, 7)], cut_recv.at[u, 1])
+        count(119, cut_recv.at[u, 0])
         summed = restore(share_send[u, cut], share_scale[u, cut])
         for o in range(1, 8):
             summed = summed + restore(share_recv[u, o], share_rscale[u, o])
@@ -373,8 +372,7 @@
                 copy.start()
 
     def stage6(u):
-        landed(mean_coded.at[u, pl.ds(0, 7)], cut_recv.at[u, 2])
-        landed(mean_scale.at[u, pl.ds(0, 7)], cut_recv.at[u, 3])
+        count(119, cut_recv.at[u, 1])
         mean[div4(u), at(base_of(u), 64, 64), :] = unfold(restore(mean_coded[u], mean_scale[u][:, None]))
 
     def step(t, _):
@@ -573,14 +571,15 @@
             dma,
             dma((4, 2)),
             dma((3, 2)),
-            dma((STEPS, 2, 2, 2)),
+            dma((STEPS, 2, 2)),
             dma((5,)),
-            dma((STEPS, 4)),
+            dma((STEPS, 2)),
             dma((2, 2)),
             dma((2, 3)),
             dma((2, 3)),
             dma((2, 2, 2)),
             pltpu.SemaphoreType.REGULAR((2,)),
+            pltpu.VMEM((1028, 1, 128), f32),
         ],
         compiler_params=pltpu.CompilerParams(
             collective_id=0, has_side_effects=True, vmem_limit_bytes=limit),

time: 85.2 us -> 84.8 us (level)
  no operation moved by 1% of the time
where the time goes in v6:
time: 84.8 us; the launch traced here: 84.6 us
  Pallas kernels  83.8 us (99%)
    pallas_call x1, Pallas kernels, body(): pl.pallas_call(exchange, out_shape=(jax.ShapeDtypeStruct((2, 256, 512), f...  78.1 us
    pallas_call x1, Pallas kernels, body(): pl.pallas_call(decompress, out_shape=(jax.ShapeDtypeStruct((2, 256, 8192)...  5.72 us

profile of v6, /device:TPU:1, one launch (start us, length us, event | category | flops | bytes accessed | tf_op | source)
XLA Modules:
  0.0 84.6 jit_solution(10307336443254477969)
XLA Ops:
  0.6 78.1 %exchange.1 = (f32[2,256,512]{2,1,0:T(8,128)}, s16[2,2,16,32,128]{4,3,2,1,0:T(8,128)(2,1)}, s16[2,2,16,2,32,128]{5,4,3,2,1,0:T(8,128)(2,1)}, f32[2,16,2,1,128]{4,3,2,1,0:T(1,128)}) custom-call(f32[2,256,8192]{2,1,0:T(8,128)} %bitcast.5, f32[2,256,512]{2,1,0:T(8,128)} %bitcast.6, s32[2,32,512]{2,1,0:T(8,128)} %bitcast.7), custom_call_target="tpu_custom_call" | custom-call | tf_op jit(solution)/shard_map/exchange/pallas_call | solution.py:544
  78.7 5.7 %decompress.1 = (bf16[2,256,8192]{2,1,0:T(8,128)(2,1)}, f32[2,256,512]{2,1,0:T(8,128)}) custom-call(s32[1]{0:T(128)} %bitcast.member_ref, s16[2,2,16,32,128]{4,3,2,1,0:T(8,128)(2,1)} %get-tuple-element.8.basis_q, s16[2,2,16,2,32,128]{5,4,3,2,1,0:T(8,128)(2,1)} %get-tuple-element.9.right_q, f32[2,16,2,1,128]{4,3,2,1,0:T(1,128)} %get-tuple-element.10.factor_s, ...), custom_call_target="tpu_custom_call" | custom-call | tf_op jit(solution)/shard_map/decompress/pallas_call | solution.py:590
